TPU v7x, 128 devices: a whole 4x4x4 slice. The times are simulated.
128 devices in a mesh: grp: 2 (over core), seq: 16 (over z, x), head: 4 (over y).
Axes of the slice: x: 4, y: 4, z: 4, core: 2. Of those that a mesh axis runs over, the one named last changes fastest.
Arguments:
- enc_in: bfloat16 [2, 4096, 1024], P('grp', 'seq'), may hold values from -6 to 6
- enc_gain: float32 [1024], replicated, may hold values from 0.1 to 1.9
- w_in: bfloat16 [1024, 4096], P(None, 'head'), may hold values from -0.1875 to 0.1875
- w_out: bfloat16 [4096, 1024], P('head'), may hold values from -0.09375 to 0.09375
- w_key: bfloat16 [1024, 2048], P(None, 'head'), may hold values from -0.1875 to 0.1875
- w_value: bfloat16 [1024, 2048], P(None, 'head'), may hold values from -0.1875 to 0.1875
- dec_in: bfloat16 [2, 4096, 4096], P('grp', 'seq'), may hold values from -16 to 16
- w_query: bfloat16 [4096, 2048], P(None, 'head'), may hold values from -0.09375 to 0.09375
- w_attn_out: bfloat16 [2048, 4096], P('head'), may hold values from -0.125 to 0.125
- cotangent: bfloat16 [2, 4096, 4096], P('grp', 'seq'), may hold values from -0.75 to 0.75
- group_doc: int32 [2, 16], P('grp'), may hold values from 0 to 7, never falling along the last dimension, each value on 1 to 5 neighbouring positions
- doc_lengths: int32 [2, 8], P('grp'), may hold values from 1 to 2048, 4096 in all within a row
Outputs:
- out: bfloat16 [2, 4096, 4096], P('grp', 'seq', 'head')
- grad_w_query: float32 [4096, 2048], P(('grp', 'seq'), 'head')
- grad_w_key: float32 [1024, 2048], P(('grp', 'seq'), 'head')
- grad_w_value: float32 [1024, 2048], P(('grp', 'seq'), 'head')
- grad_w_attn_out: float32 [2048, 4096], P('head', ('grp', 'seq'))
- grad_w_in: float32 [1024, 4096], P(('grp', 'seq'), 'head')
- grad_w_out: float32 [4096, 1024], P('head', ('grp', 'seq'))
Inputs may be any that keep to these rules, and one draw needn't show every extreme that they name: `group_doc`: never falls along a sequence; each of the 8 documents owns at least one group. `doc_lengths`: the lengths of a sequence sum to 4096; the largest is exactly 2048.
All inputs are finite; a program needn't handle non-finite values.
Results may differ from a plain program's by a relative error of at most 0.029.
Values may be sent and summed in bfloat16 or wider, within the bound.
A program may use at most 128 MiB of HBM per device.

v0:
```python
import math

import jax
import jax.numpy as jnp
from jax import lax
from jax.sharding import PartitionSpec as P

HEAD_DIM = 128
GROUP = 256


epsilon = 1e-06
masked_score = -1e30


def matmul(left_side, right_side):
    return jnp.dot(left_side, right_side, preferred_element_type=jnp.float32)


def inner_rows(left_side, right_side):
    return lax.dot_general(
        left_side, right_side, (((0,), (0,)), ((), ())), preferred_element_type=jnp.float32
    )


def inner_cols(left_side, right_side):
    return lax.dot_general(
        left_side, right_side, (((1,), (1,)), ((), ())), preferred_element_type=jnp.float32
    )


def silu_slope(argument):
    sigmoid_v = jax.nn.sigmoid(argument)
    return sigmoid_v * (1.0 + argument * (1.0 - sigmoid_v))


def split_heads(matrix, head_width):
    return matrix.reshape(matrix.shape[0], -1, head_width).transpose(1, 0, 2)


def join_heads(stacked):
    return stacked.transpose(1, 0, 2).reshape(stacked.shape[1], -1)


def one_head(query_rows, key_rows, value_rows, d_mixed, allowed, score_scale):
    scores = inner_cols(query_rows, key_rows) * score_scale
    scores = jnp.where(allowed, scores, masked_score)
    row_max = jnp.max(scores, axis=1, keepdims=True)
    exp_scores = jnp.exp(scores - row_max)
    probabilities = exp_scores / jnp.sum(exp_scores, axis=1, keepdims=True)
    attn_weights = probabilities.astype(jnp.bfloat16)
    mixed_rows = matmul(attn_weights, value_rows)
    d_weights = inner_cols(d_mixed, value_rows)
    inner_sum = jnp.sum(probabilities * d_weights, axis=1, keepdims=True)
    d_scores = (probabilities * (d_weights - inner_sum) * score_scale).astype(jnp.bfloat16)
    d_query = matmul(d_scores, key_rows)
    d_key = inner_rows(d_scores, query_rows)
    d_value = inner_rows(attn_weights, d_mixed)
    return (mixed_rows, d_query, d_key, d_value)


def attend(queries, all_keys, values, d_mixed, allowed):
    score_scale = 1.0 / math.sqrt(HEAD_DIM)

    def per_head(head_items):
        return one_head(
            head_items[0], head_items[1], head_items[2], head_items[3], allowed, score_scale
        )

    stacked = lax.map(
        per_head,
        (
            split_heads(queries, HEAD_DIM),
            split_heads(all_keys, HEAD_DIM),
            split_heads(values, HEAD_DIM),
            split_heads(d_mixed, HEAD_DIM),
        ),
    )
    return (
        join_heads(stacked[0]),
        join_heads(stacked[1]),
        join_heads(stacked[2]),
        join_heads(stacked[3]),
    )


def shards(
    enc_in,
    enc_gain,
    w_in,
    w_out,
    w_key,
    w_value,
    dec_in,
    w_query,
    w_attn_out,
    cotangent,
    group_doc,
    doc_lengths,
):
    encoded = enc_in[0].astype(jnp.float32)
    square = jnp.mean(encoded * encoded, axis=1, keepdims=True)
    normed = (encoded * lax.rsqrt(square + epsilon) * enc_gain).astype(jnp.bfloat16)
    pre_act = matmul(normed, w_in)
    activated = jax.nn.silu(pre_act).astype(jnp.bfloat16)
    summed = lax.psum(matmul(activated, w_out), "head")
    enc_out = (encoded + summed).astype(jnp.bfloat16)
    keys_own = matmul(enc_out, w_key).astype(jnp.bfloat16)
    values_own = matmul(enc_out, w_value).astype(jnp.bfloat16)
    all_keys, values = (
        lax.all_gather(keys_own, "seq", axis=0, tiled=True),
        lax.all_gather(values_own, "seq", axis=0, tiled=True),
    )
    decoder = dec_in[0]
    upstream = cotangent[0]
    row_count = decoder.shape[0]
    positions = lax.axis_index("seq") * row_count + jnp.arange(row_count, dtype=jnp.int32)
    doc_ends = jnp.cumsum(doc_lengths[0])
    query_doc = jnp.sum((positions[:, None] >= doc_ends[None, :]).astype(jnp.int32), axis=1)
    key_doc = jnp.repeat(group_doc[0], GROUP)
    allowed = query_doc[:, None] == key_doc[None, :]
    queries = matmul(decoder, w_query).astype(jnp.bfloat16)
    d_mixed = inner_cols(upstream, w_attn_out).astype(jnp.bfloat16)
    mixed_f, d_query, d_key, d_value = attend(queries, all_keys, values, d_mixed, allowed)
    mixed_b = mixed_f.astype(jnp.bfloat16)
    partial_out = matmul(mixed_b, w_attn_out)
    col_width = decoder.shape[1] // lax.axis_size("head")
    residual = lax.dynamic_slice_in_dim(
        decoder, lax.axis_index("head") * col_width, col_width, 1
    ).astype(jnp.float32)
    own_share = lax.psum_scatter(partial_out, "head", scatter_dimension=1, tiled=True)
    result = (residual + own_share).astype(jnp.bfloat16)[None]
    own_key, own_value = (
        lax.psum_scatter(d_key.astype(jnp.bfloat16), "seq", scatter_dimension=0, tiled=True).astype(
            jnp.float32
        ),
        lax.psum_scatter(
            d_value.astype(jnp.bfloat16), "seq", scatter_dimension=0, tiled=True
        ).astype(jnp.float32),
    )
    key_grad = own_key.astype(jnp.bfloat16)
    value_grad = own_value.astype(jnp.bfloat16)
    d_enc = lax.psum(inner_cols(key_grad, w_key) + inner_cols(value_grad, w_value), "head")
    d_enc_b = d_enc.astype(jnp.bfloat16)
    d_pre = (inner_cols(d_enc_b, w_out) * silu_slope(pre_act)).astype(jnp.bfloat16)
    d_query_b = d_query.astype(jnp.bfloat16)
    g_query, g_key, g_value, g_in = (
        lax.psum_scatter(
            inner_rows(decoder, d_query_b).astype(jnp.bfloat16),
            ("grp", "seq"),
            scatter_dimension=0,
            tiled=True,
        ).astype(jnp.float32),
        lax.psum_scatter(
            inner_rows(enc_out, key_grad).astype(jnp.bfloat16),
            ("grp", "seq"),
            scatter_dimension=0,
            tiled=True,
        ).astype(jnp.float32),
        lax.psum_scatter(
            inner_rows(enc_out, value_grad).astype(jnp.bfloat16),
            ("grp", "seq"),
            scatter_dimension=0,
            tiled=True,
        ).astype(jnp.float32),
        lax.psum_scatter(
            inner_rows(normed, d_pre).astype(jnp.bfloat16),
            ("grp", "seq"),
            scatter_dimension=0,
            tiled=True,
        ).astype(jnp.float32),
    )
    g_attn, g_out = (
        lax.psum_scatter(
            inner_rows(mixed_b, upstream).astype(jnp.bfloat16),
            ("grp", "seq"),
            scatter_dimension=1,
            tiled=True,
        ).astype(jnp.float32),
        lax.psum_scatter(
            inner_rows(activated, d_enc_b).astype(jnp.bfloat16),
            ("grp", "seq"),
            scatter_dimension=1,
            tiled=True,
        ).astype(jnp.float32),
    )
    return (result, g_query, g_key, g_value, g_attn, g_in, g_out)


def solution(mesh):
    placed = (
        P("grp", "seq", None),
        P(),
        P(None, "head"),
        P("head", None),
        P(None, "head"),
        P(None, "head"),
        P("grp", "seq", None),
        P(None, "head"),
        P("head", None),
        P("grp", "seq", None),
        P("grp", None),
        P("grp", None),
    )
    return jax.shard_map(
        shards,
        mesh=mesh,
        in_specs=placed,
        out_specs=(
            P("grp", "seq", "head"),
            P(("grp", "seq"), "head"),
            P(("grp", "seq"), "head"),
            P(("grp", "seq"), "head"),
            P("head", ("grp", "seq")),
            P(("grp", "seq"), "head"),
            P("head", ("grp", "seq")),
        ),
        check_vma=False,
    )
```

profile of v0, /device:TPU:0, one launch (start us, length us, event | category | flops | bytes accessed | tf_op | source)
XLA Modules:
  0.0 949.1 jit_solution(1043757524598367171)
XLA Ops:
  8.6 2.5 fusion.71
  14.0 48.3 %all-reduce.3.cloned.1.call-done = f32[256,1024]{1,0:T(8,128)} async-done(((f32[256,1024]{1,0:T(8,128)}), f32[256,1024]{1,0:T(8,128)}) %all-reduce.3.cloned.1.call-update) | async-done | bytes 1048592 | tf_op jit(solution)/shard_map/psum | solution.py:106
  69.0 3.6 fusion.50
  75.1 43.6 %all-gather.5.cloned.1.call-done = bf16[4096,512]{1,0:T(8,128)(2,1)} async-done(((bf16[256,512]{1,0:T(8,128)(2,1)}), bf16[4096,512]{1,0:T(8,128)(2,1)}) %all-gather.5.cloned.1.call-update) | async-done | bytes 4194320 | tf_op jit(solution)/shard_map/all_gather | solution.py:112
  118.7 5.0 bitcast_bitcast_fusion
  123.7 48.7 %all-gather.3.cloned.1.call-done = bf16[4096,512]{1,0:T(8,128)(2,1)} async-done(((bf16[256,512]{1,0:T(8,128)(2,1)}), bf16[4096,512]{1,0:T(8,128)(2,1)}) %all-gather.3.cloned.1.call-update) | async-done | bytes 4194320 | tf_op jit(solution)/shard_map/all_gather | solution.py:111
  172.4 4.8 bitcast_bitcast_fusion.1
  177.2 61.9 %while.17 = (s32[]{:T(128)}, bf16[4,256,128]{1,2,0:T(8,128)(2,1)S(1)}, bf16[4,256,128]{1,2,0:T(8,128)(2,1)}, bf16[4,4096,128]{1,2,0:T(8,128)(2,1)}, bf16[4,4096,...) while((s32[]{:T(128)}, ...), condition=%wide.region_8.9_spmd.clone, body=%wide.region_4.8_spmd.clone.sunk | while | flops 1633680640 | bytes 135827824 | solution.py:70
  188.0 2.9 fusion.130
  203.4 2.9 fusion.130
  218.9 2.9 fusion.130
  234.4 2.9 fusion.130
  240.0 3.2 convolution_convert_fusion
  243.1 6.6 copy.53
  249.9 4.9 fusion.36
  254.8 6.5 copy.51
  261.4 5.6 fusion.76
  267.0 49.6 %reduce-scatter.16.cloned.1.call-done = bf16[256,512]{0,1:T(8,128)(2,1)} async-done(((bf16[4096,512]{0,1:T(8,128)(2,1)}), bf16[256,512]{0,1:T(8,128)(2,1)}) %reduce-scatter.16.cloned.1.call-update) | async-done | bytes 262160 | tf_op jit(solution)/shard_map/reduce_scatter | solution.py:134
  316.6 2.5 convolution_convert_fusion.5
  319.2 77.6 %reduce-scatter.20.cloned.1.call-done = bf16[256,512]{0,1:T(8,128)(2,1)} async-done(((bf16[4096,512]{0,1:T(8,128)(2,1)}), bf16[256,512]{0,1:T(8,128)(2,1)}) %reduce-scatter.20.cloned.1.call-update) | async-done | bytes 262160 | tf_op jit(solution)/shard_map/reduce_scatter | solution.py:137
  396.8 2.4 convolution_convert_fusion.4
  401.1 2.8 convolution_add_fusion
  403.9 33.2 %all-reduce.4 = bf16[256,1024]{1,0:T(8,128)(2,1)S(1)} all-reduce(f32[256,1024]{1,0:T(8,128)} %convolution_add_fusion), channel_id=1, replica_groups=mesh['grp'=2,'seq'=16,'head'=4] {'head'}, use_global_device_ids=true, to_apply=%region_16.17 | all-reduce | flops 262144 | bytes 1572864 | tf_op jit(solution)/shard_map/psum | solution.py:143
  437.1 4.6 convolution_convert_fusion.3
  441.8 3.4 convolution_convert_fusion.2
  445.2 37.0 %reduce-scatter.30.cloned.1.call-done = bf16[128,512]{1,0:T(8,128)(2,1)} async-done(((bf16[4096,512]{1,0:T(8,128)(2,1)}), bf16[128,512]{1,0:T(8,128)(2,1)}) %reduce-scatter.30.cloned.1.call-update) | async-done | bytes 131088
  483.9 83.2 %reduce-scatter.28.cloned.1.call-done = bf16[128,512]{1,0:T(8,128)(2,1)} async-done(((bf16[4096,512]{1,0:T(8,128)(2,1)}), bf16[128,512]{1,0:T(8,128)(2,1)}) %reduce-scatter.28.cloned.1.call-update) | async-done | bytes 131088
  569.0 46.8 %reduce-scatter.14.cloned.1.call-done = f32[256,1024]{1,0:T(8,128)} async-done(((f32[256,4096]{1,0:T(8,128)}), f32[256,1024]{1,0:T(8,128)}) %reduce-scatter.14.cloned.1.call-update) | async-done | bytes 1048592 | tf_op jit(solution)/shard_map/reduce_scatter | solution.py:131
  618.1 78.6 %reduce-scatter.18.cloned.1.call-done = bf16[32,512]{1,0:T(8,128)(2,1)} async-done(((bf16[1024,512]{1,0:T(8,128)(2,1)}), bf16[32,512]{1,0:T(8,128)(2,1)}) %reduce-scatter.18.cloned.1.call-update) | async-done | bytes 32784 | tf_op jit(solution)/shard_map/reduce_scatter | solution.py:154
  698.1 79.3 %reduce-scatter.22.cloned.1.call-done = bf16[32,512]{1,0:T(8,128)(2,1)} async-done(((bf16[1024,512]{1,0:T(8,128)(2,1)}), bf16[32,512]{1,0:T(8,128)(2,1)}) %reduce-scatter.22.cloned.1.call-update) | async-done | bytes 32784 | tf_op jit(solution)/shard_map/reduce_scatter | solution.py:160
  778.7 80.4 %reduce-scatter.24.cloned.1.call-done = bf16[32,1024]{1,0:T(8,128)(2,1)} async-done(((bf16[1024,1024]{1,0:T(8,128)(2,1)}), bf16[32,1024]{1,0:T(8,128)(2,1)}) %reduce-scatter.24.cloned.1.call-update) | async-done | bytes 65552 | tf_op jit(solution)/shard_map/reduce_scatter | solution.py:166
  860.6 80.1 %reduce-scatter.26.cloned.1.call-done = bf16[1024,32]{0,1:T(8,128)(2,1)} async-done(((bf16[1024,1024]{0,1:T(8,128)(2,1)}), bf16[1024,32]{0,1:T(8,128)(2,1)}) %reduce-scatter.26.cloned.1.call-update) | async-done | bytes 65552 | tf_op jit(solution)/shard_map/reduce_scatter | solution.py:180
  (167 shorter events, 77.7 us)
Async XLA Ops:
  7.2 61.9 %copy-start = (bf16[1,256,4096]{2,1,0:T(8,128)(2,1)S(1)}, bf16[1,256,4096]{2,1,0:T(8,128)(2,1)}, u32[]{:S(2)}) copy-start(bf16[1,256,4096]{2,1,0:T(8,128)(2,1)} %param.23) | copy-start | bytes 6291460
  7.2 55.1 %all-reduce.3.cloned.1.call-start = ((), (), s32[]{:S(2)}) async-start(), calls=%async_computation.9 | async-start | bytes 2097152 | tf_op jit(solution)/shard_map/psum | solution.py:106
  7.2 4.9 copy-start.18
  8.6 5.3 copy-start.13
  12.1 50.1 %copy-start.1 = (bf16[1,256,1024]{2,1,0:T(8,128)(2,1)S(1)}, bf16[1,256,1024]{2,1,0:T(8,128)(2,1)}, u32[]{:S(2)}) copy-start(bf16[1,256,1024]{2,1,0:T(8,128)(2,1)} %param.14) | copy-start | bytes 1572868
  13.9 54.7 %copy-start.19 = (s32[1,8]{1,0:T(1,128)S(1)}, s32[1,8]{1,0:T(1,128)}, u32[]{:S(2)}) copy-start(s32[1,8]{1,0:T(1,128)} %param.25) | copy-start | bytes 100
  13.9 54.9 %copy-start.16 = (s32[1,16]{1,0:T(1,128)S(1)}, s32[1,16]{1,0:T(1,128)}, u32[]{:S(2)}) copy-start(s32[1,16]{1,0:T(1,128)} %param.24) | copy-start | bytes 196
  13.9 104.8 %all-gather.5.cloned.1.call-start = ((), (), s32[]{:S(2)}) async-start(), calls=%async_computation.11 | async-start | bytes 4456448 | tf_op jit(solution)/shard_map/all_gather | solution.py:112
  66.1 106.3 %all-gather.3.cloned.1.call-start = ((), (), s32[]{:S(2)}) async-start(), calls=%async_computation.10 | async-start | bytes 4456448 | tf_op jit(solution)/shard_map/all_gather | solution.py:111
  68.5 248.1 %reduce-scatter.16.cloned.1.call-start = ((), (), s32[]{:S(2)}) async-start(), calls=%async_computation.13 | async-start | bytes 4456448 | tf_op jit(solution)/shard_map/reduce_scatter | solution.py:134
  68.9 3.8 copy-start.7
  68.9 4.1 copy-start.17
  180.2 3.0 copy-start.2
  192.7 3.0 copy-start.5
  192.7 3.0 copy-start.12
  195.7 3.0 copy-start.2
  208.1 3.0 copy-start.5
  208.2 3.0 copy-start.12
  211.2 3.0 copy-start.2
  223.6 3.0 copy-start.5
  226.7 3.0 copy-start.2
  239.1 157.7 %reduce-scatter.20.cloned.1.call-start = ((), (), s32[]{:S(2)}) async-start(), calls=%async_computation.15 | async-start | bytes 4456448 | tf_op jit(solution)/shard_map/reduce_scatter | solution.py:137
  239.7 242.4 %reduce-scatter.30.cloned.1.call-start = ((), (), s32[]{:S(2)}) async-start(), calls=%async_computation.20 | async-start | bytes 4325376
  249.8 317.3 %reduce-scatter.28.cloned.1.call-start = ((), (), s32[]{:S(2)}) async-start(), calls=%async_computation.19 | async-start | bytes 4325376
  261.3 354.5 %reduce-scatter.14.cloned.1.call-start = ((), (), s32[]{:S(2)}) async-start(), calls=%async_computation.12 | async-start | bytes 5242880 | tf_op jit(solution)/shard_map/reduce_scatter | solution.py:131
  267.0 429.7 %reduce-scatter.18.cloned.1.call-start = ((), (), s32[]{:S(2)}) async-start(), calls=%async_computation.14 | async-start | bytes 1081344 | tf_op jit(solution)/shard_map/reduce_scatter | solution.py:154
  316.6 82.7 %copy-start.8 = (bf16[256,512]{0,1:T(8,128)(2,1)S(1)}, bf16[256,512]{0,1:T(8,128)(2,1)}, u32[]{:S(2)}) copy-start(bf16[256,512]{0,1:T(8,128)(2,1)} %reduce-scatter.16.cloned.1.call-done) | copy-start | bytes 786436
  319.1 458.2 %reduce-scatter.22.cloned.1.call-start = ((), (), s32[]{:S(2)}) async-start(), calls=%async_computation.16 | async-start | bytes 1081344 | tf_op jit(solution)/shard_map/reduce_scatter | solution.py:160
  399.3 37.8 %copy-start.14 = (f32[256]{0:T(256)S(1)}, f32[256]{0:T(256)}, u32[]{:S(2)}) copy-start(f32[256]{0:T(256)} %copy-done.13) | copy-start | bytes 3076
  399.3 37.8 %copy-start.15 = (f32[1024]{0:T(1024)S(1)}, f32[1024]{0:T(1024)}, u32[]{:S(2)}) copy-start(f32[1024]{0:T(1024)} %param.15) | copy-start | bytes 12292
  399.3 459.8 %reduce-scatter.24.cloned.1.call-start = ((), (), s32[]{:S(2)}) async-start(), calls=%async_computation.17 | async-start | bytes 2162688 | tf_op jit(solution)/shard_map/reduce_scatter | solution.py:166
  441.7 499.1 %reduce-scatter.26.cloned.1.call-start = ((), (), s32[]{:S(2)}) async-start(), calls=%async_computation.18 | async-start | bytes 2162688 | tf_op jit(solution)/shard_map/reduce_scatter | solution.py:180
  (24 other events, 47.9 us)
Sparse Core Ops, SparseCore 0:
  14.0 48.2 all-reduce.2
  66.2 52.4 all-gather.4
  121.1 51.2 all-gather.2
  239.3 77.3 reduce-scatter.15
  319.8 76.9 reduce-scatter.19
  400.8 81.3 reduce-scatter.29
  485.8 81.2 reduce-scatter.27
  569.7 46.0 reduce-scatter.13
  619.3 77.3 reduce-scatter.17
  700.4 76.8 reduce-scatter.21
  780.9 78.2 reduce-scatter.23
  862.5 78.1 reduce-scatter.25
where the time goes:
time: 951 us; the launch traced here: 949 us
  waiting for transfers between devices  754 us (79%)
  matrix products  84.1 us (9%)
  local copies, waits for them, and re-layouts  40.2 us (4%)
  blocking collectives  33.2 us (3%)
  other arithmetic  22.1 us (2%)
  between operations  14.4 us (2%)
    unnamed x14, waiting for transfers between devices  121 us
    reduce_scatter x1, waiting for transfers between devices, shards(): lax.psum_scatter(inner_rows(normed, d_pre).astype(jnp.bfloat16), ('grp',...  80.4 us
    reduce_scatter x1, waiting for transfers between devices, shards(): lax.psum_scatter(inner_rows(activated, d_enc_b).astype(jnp.bfloat16), ('g...  80.1 us
    reduce_scatter x1, waiting for transfers between devices, shards(): lax.psum_scatter(inner_rows(enc_out, value_grad).astype(jnp.bfloat16), ('...  79.3 us
    reduce_scatter x1, waiting for transfers between devices, shards(): lax.psum_scatter(inner_rows(enc_out, key_grad).astype(jnp.bfloat16), ('gr...  78.6 us
    reduce_scatter x1, waiting for transfers between devices, shards(): lax.psum_scatter(d_value.astype(jnp.bfloat16), 'seq', scatter_dimension=0...  77.6 us
    reduce_scatter x1, waiting for transfers between devices, shards(): lax.psum_scatter(d_key.astype(jnp.bfloat16), 'seq', scatter_dimension=0,...  49.6 us
    all_gather x1, waiting for transfers between devices, shards(): lax.all_gather(keys_own, 'seq', axis=0, tiled=True)  48.7 us
  transfers between devices with their start and end apart: 12, of which 12 were waited for; matrix products, arithmetic and copies ran while one was open for 7% of the time, Pallas kernels for 0%

commit v1 on v0

v1 whole, which is shorter than its diff:
```python
import functools
import math

import jax
import jax.numpy as jnp
from jax import lax
from jax.experimental import pallas as pl
from jax.experimental.pallas import tpu as pltpu
from jax.sharding import PartitionSpec as P

HEAD_DIM = 128
GROUP = 256
N_SEQ = 16
N_HEAD = 4
EPSILON = 1e-06
MASKED = -1e30
SCALE = 1.0 / math.sqrt(HEAD_DIM)
MESH = pl.DeviceIdType.MESH
BF = jnp.bfloat16
F32 = jnp.float32
VMEM_LIMIT = 62 * 1024 * 1024
VM = pl.BlockSpec(memory_space=pltpu.VMEM)
ANY = pl.BlockSpec(memory_space=pl.ANY)


def mm(a, b):
    return lax.dot_general(a, b, (((1,), (0,)), ((), ())), preferred_element_type=F32)


def mm_rows(a, b):
    return lax.dot_general(a, b, (((0,), (0,)), ((), ())), preferred_element_type=F32)


def mm_cols(a, b):
    return lax.dot_general(a, b, (((1,), (1,)), ((), ())), preferred_element_type=F32)


def ring_pos(lane, s):
    z, x = lax.div(s, 4), lax.rem(s, 4)
    w = lax.rem(x + z, 4)
    p = 4 * z + w if lane < 2 else 4 * x + w
    return p if lane % 2 == 0 else lax.rem(16 - p, 16)


def ring_dev(lane, p):
    if lane % 2 == 1:
        p = lax.rem(16 - p, 16)
    a = lax.div(p, 4)
    b = lax.rem(lax.rem(p, 4) + 4 - a, 4)
    return 4 * a + b if lane < 2 else 4 * b + a


class Rings:
    def __init__(self, rows, send_sem, recv_sem):
        s = lax.axis_index("seq")
        self.rows = rows
        self.pos = [ring_pos(q, s) for q in range(4)]
        self.next = [ring_dev(q, lax.rem(self.pos[q] + 1, 16)) for q in range(4)]
        self.me = s
        self.ss, self.rs = send_sem, recv_sem

    def part(self, q):
        return pl.ds(q * self.rows, self.rows)

    def dev(self, q, back):
        return ring_dev(q, lax.rem(self.pos[q] + 32 - back, 16))

    def copy(self, q, t, src, dst):
        return pltpu.make_async_remote_copy(
            src_ref=src,
            dst_ref=dst,
            send_sem=self.ss.at[q, t],
            recv_sem=self.rs.at[q, t],
            device_id={"seq": self.next[q]},
            device_id_type=MESH,
        )


class Gather(Rings):
    def __init__(self, blocks, rows, ss, rs):
        super().__init__(rows, ss, rs)
        self.blocks = blocks

    def sending(self, q, t):
        ref = self.blocks.at[self.dev(q, t), self.part(q)]
        return self.copy(q, t, ref, ref)

    def landing(self, q, t):
        ref = self.blocks.at[self.dev(q, t + 1), self.part(q)]
        return self.copy(q, t, ref, ref)

    def start(self):
        for q in range(4):
            self.sending(q, 0).start()

    def step(self, t):
        for q in range(4):
            self.landing(q, t).wait_recv()
            self.sending(q, t + 1).start()

    def finish(self):
        for q in range(4):
            self.landing(q, 14).wait_recv()

    def drain(self):
        def body(t, c):
            for q in range(4):
                self.sending(q, t).wait_send()
            return c

        lax.fori_loop(0, 15, body, 0)


class Scatter(Rings):
    def __init__(self, blocks, slots, rows, ss, rs):
        super().__init__(rows, ss, rs)
        self.blocks, self.slots = blocks, slots

    def start(self):
        for q in range(4):
            src = self.blocks.at[self.dev(q, 1), self.part(q)]
            self.copy(q, 0, src, self.slots.at[q, 0]).start()

    def sending(self, q, t):
        return self.copy(q, t + 1, self.slots.at[q, t], self.slots.at[q, t + 1])

    def landing(self, q, t):
        return self.copy(q, t, self.slots.at[q, t], self.slots.at[q, t])

    def step(self, t):
        for q in range(4):
            self.landing(q, t).wait_recv()
            own = self.blocks[self.dev(q, t + 2), self.part(q)]
            self.slots[q, t] = (self.slots[q, t].astype(F32) + own.astype(F32)).astype(BF)
            self.sending(q, t).start()

    def finish(self, q):
        self.landing(q, 14).wait_recv()
        own = self.blocks[self.me, self.part(q)]
        return self.slots[q, 14].astype(F32) + own.astype(F32)

    def drain(self):
        for q in range(4):
            src = self.blocks.at[self.dev(q, 1), self.part(q)]
            self.copy(q, 0, src, self.slots.at[q, 0]).wait_send()

        def body(t, c):
            for q in range(4):
                self.sending(q, t).wait_send()
            return c

        lax.fori_loop(0, 14, body, 0)


def greet(with_partner):
    s = lax.axis_index("seq")
    h = lax.axis_index("head")
    barrier = pltpu.get_barrier_semaphore()
    count = 0
    for q in range(4):
        right = ring_dev(q, lax.rem(ring_pos(q, s) + 1, 16))
        pl.semaphore_signal(barrier, inc=1, device_id={"seq": right}, device_id_type=MESH)
        count += 1
    for d in range(1, 4):
        pl.semaphore_signal(
            barrier, inc=1, device_id={"head": lax.rem(h + d, 4)}, device_id_type=MESH
        )
        count += 1
    if with_partner:
        pl.semaphore_signal(
            barrier, inc=1, device_id={"grp": 1 - lax.axis_index("grp")}, device_id_type=MESH
        )
        count += 1
    pl.semaphore_wait(barrier, count)


def head_copy(d, src, dst, ss, rs):
    h = lax.axis_index("head")
    return pltpu.make_async_remote_copy(
        src_ref=src,
        dst_ref=dst,
        send_sem=ss.at[d - 1],
        recv_sem=rs.at[d - 1],
        device_id={"head": lax.rem(h + d, 4)},
        device_id_type=MESH,
    )


class HeadSum:
    def __init__(self, parts, slots, total, ss, rs, ss2, rs2):
        self.parts, self.slots, self.total = parts, slots, total
        self.ss, self.rs, self.ss2, self.rs2 = ss, rs, ss2, rs2
        self.h = lax.axis_index("head")

    def quarter(self, h):
        return pl.ds(pl.multiple_of(h * 64, 64), 64)

    def first(self, d):
        src = self.parts.at[self.quarter(lax.rem(self.h + d, 4))]
        return head_copy(d, src, self.slots.at[d - 1], self.ss, self.rs)

    def second(self, d):
        ref = self.total.at[self.quarter(self.h)]
        return head_copy(d, ref, ref, self.ss2, self.rs2)

    def second_landing(self, d):
        ref = self.total.at[self.quarter(lax.rem(self.h + 4 - d, 4))]
        return head_copy(d, ref, ref, self.ss2, self.rs2)

    def send(self):
        for d in (2, 1, 3):
            self.first(d).start()

    def receive(self):
        total = self.parts[self.quarter(self.h)].astype(F32)
        for d in (1, 3, 2):
            self.first(d).wait_recv()
            total = total + self.slots[d - 1].astype(F32)
        return total

    def share(self, total):
        self.total[self.quarter(self.h)] = total.astype(BF)
        for d in (2, 1, 3):
            self.second(d).start()

    def collect(self):
        for d in (1, 3, 2):
            self.second_landing(d).wait_recv()

    def drain(self):
        for d in (1, 2, 3):
            self.first(d).wait_send()
            self.second(d).wait_send()


def encoder_kernel(
    enc_in, gain, w_in, w_out, w_key, w_value, dec, w_query, w_attn, cot,
    normed, pre_act, activated, enc_out, kv, queries, d_mixed,
    v_in, v_out, v_key, v_value, v_dec, v_query, v_attn, v_cot, load_sem,
    parts, slots, hs1, hr1, hs2, hr2, ring_s, ring_r,
):
    pairs = (
        (w_in, v_in), (w_out, v_out), (dec, v_dec), (w_query, v_query),
        (w_key, v_key), (w_value, v_value), (cot, v_cot), (w_attn, v_attn),
    )
    loads = {id(v): pltpu.make_async_copy(a, v, load_sem.at[i]) for i, (a, v) in enumerate(pairs)}
    for copy in loads.values():
        copy.start()
    greet(False)
    seq = lax.axis_index("seq")
    encoded = enc_in[...].astype(F32)
    square = jnp.mean(encoded * encoded, axis=1, keepdims=True)
    normed[...] = (encoded * lax.rsqrt(square + EPSILON) * gain[...]).astype(BF)
    loads[id(v_in)].wait()
    for n in range(4):
        cols = pl.ds(n * 256, 256)
        pre = mm(normed[...], v_in[:, cols])
        pre_act[:, cols] = pre
        activated[:, cols] = (pre / (1.0 + jnp.exp(-pre))).astype(BF)
    loads[id(v_out)].wait()
    for n in range(4):
        cols = pl.ds(n * 256, 256)
        parts[:, cols] = mm(activated[...], v_out[:, cols]).astype(BF)
    across = HeadSum(parts, slots, enc_out, hs1, hr1, hs2, hr2)
    across.send()
    loads[id(v_dec)].wait()
    loads[id(v_query)].wait()
    for n in range(2):
        cols = pl.ds(n * 256, 256)
        queries[:, cols] = mm(v_dec[...], v_query[:, cols]).astype(BF)
    own_rows = across.quarter(across.h)
    across.share(across.receive() + enc_in[own_rows].astype(F32))
    loads[id(v_cot)].wait()
    loads[id(v_attn)].wait()
    for n in range(2):
        cols = pl.ds(n * 256, 256)
        d_mixed[:, cols] = mm_cols(v_cot[...], v_attn[cols, :]).astype(BF)
    loads[id(v_key)].wait()
    loads[id(v_value)].wait()
    across.collect()
    for n in range(2):
        cols = pl.ds(n * 256, 256)
        kv[seq, :, cols] = mm(enc_out[...], v_key[:, cols]).astype(BF)
        kv[seq, :, pl.ds(512 + n * 256, 256)] = mm(enc_out[...], v_value[:, cols]).astype(BF)
    ring = Gather(kv, 64, ring_s, ring_r)
    ring.start()

    def body(t, c):
        ring.step(t)
        return c

    lax.fori_loop(0, 14, body, 0)
    ring.finish()
    ring.drain()
    across.drain()


def run_encoder(*args):
    sds = jax.ShapeDtypeStruct
    dma = pltpu.SemaphoreType.DMA
    return pl.pallas_call(
        encoder_kernel,
        out_shape=(
            sds((256, 1024), BF), sds((256, 1024), F32), sds((256, 1024), BF), sds((256, 1024), BF),
            sds((16, 256, 1024), BF), sds((256, 512), BF), sds((256, 512), BF),
        ),
        in_specs=[VM, VM] + [ANY] * 8,
        out_specs=(VM,) * 7,
        scratch_shapes=[
            pltpu.VMEM((1024, 1024), BF), pltpu.VMEM((1024, 1024), BF),
            pltpu.VMEM((1024, 512), BF), pltpu.VMEM((1024, 512), BF),
            pltpu.VMEM((256, 4096), BF), pltpu.VMEM((4096, 512), BF),
            pltpu.VMEM((512, 4096), BF), pltpu.VMEM((256, 4096), BF), dma((8,)),
            pltpu.VMEM((256, 1024), BF), pltpu.VMEM((3, 64, 1024), BF),
            dma((3,)), dma((3,)), dma((3,)), dma((3,)), dma((4, 15)), dma((4, 15)),
        ],
        compiler_params=pltpu.CompilerParams(
            collective_id=0, has_side_effects=True, vmem_limit_bytes=VMEM_LIMIT
        ),
        cost_estimate=pl.CostEstimate(flops=5 * 10**9, bytes_accessed=30 * 2**20, transcendentals=2**18),
        name="encoder_gather",
    )(*args)


def attention_kernel(
    bounds, key_doc, query_doc, queries, d_mixed, kv_hbm, mixed, d_query, d_kv, kv, scores, acc, load_sem
):
    lo, hi = bounds[0], bounds[1]

    def load(g):
        return pltpu.make_async_copy(kv_hbm.at[g], kv.at[g], load_sem.at[g])

    def begin(g, c):
        load(g).start()
        return c

    lax.fori_loop(lo, hi, begin, 0)

    def clear(g, c):
        @pl.when((g < lo) | (g >= hi))
        def _():
            d_kv[g] = jnp.zeros((GROUP, 1024), BF)

        return c

    lax.fori_loop(0, N_SEQ, clear, 0)

    def arrive(g, c):
        load(g).wait()
        return c

    lax.fori_loop(lo, hi, arrive, 0)
    docs = query_doc[...]
    for head in range(4):
        cols = pl.ds(head * 128, 128)
        vals = pl.ds(512 + head * 128, 128)

        def score(g, m):
            s = mm_cols(queries[:, cols], kv[g, :, cols]) * SCALE
            s = jnp.where(docs == key_doc[g], s, MASKED)
            scores[g] = s
            return jnp.maximum(m, jnp.max(s, axis=1, keepdims=True))

        top = lax.fori_loop(lo, hi, score, jnp.full((256, 1), MASKED, F32))
        acc[...] = jnp.zeros((256, 128), F32)

        def weigh(g, total):
            p = jnp.exp(scores[g] - top)
            scores[g] = p
            acc[...] += mm(p.astype(BF), kv[g, :, vals])
            return total + jnp.sum(p, axis=1, keepdims=True)

        total = lax.fori_loop(lo, hi, weigh, jnp.zeros((256, 1), F32))
        inverse = 1.0 / total
        rows = acc[...] * inverse
        mixed[:, cols] = rows.astype(BF)
        inner = jnp.sum(rows * d_mixed[:, cols].astype(F32), axis=1, keepdims=True)
        acc[...] = jnp.zeros((256, 128), F32)

        def back(g, c):
            p = scores[g] * inverse
            dw = mm_cols(d_mixed[:, cols], kv[g, :, vals])
            ds = (p * (dw - inner) * SCALE).astype(BF)
            acc[...] += mm(ds, kv[g, :, cols])
            d_kv[g, :, cols] = mm_rows(ds, queries[:, cols]).astype(BF)
            d_kv[g, :, vals] = mm_rows(p.astype(BF), d_mixed[:, cols]).astype(BF)
            return c

        lax.fori_loop(lo, hi, back, 0)
        d_query[:, cols] = acc[...].astype(BF)


def run_attention(bounds, key_doc, query_doc, queries, d_mixed, kv):
    sds = jax.ShapeDtypeStruct
    smem = pl.BlockSpec(memory_space=pltpu.SMEM)
    return pl.pallas_call(
        attention_kernel,
        out_shape=(sds((256, 512), BF), sds((256, 512), BF), sds((16, 256, 1024), BF)),
        in_specs=[smem, smem, VM, VM, VM, ANY],
        out_specs=(VM,) * 3,
        scratch_shapes=[
            pltpu.VMEM((16, 256, 1024), BF), pltpu.VMEM((16, 256, 256), F32),
            pltpu.VMEM((256, 128), F32), pltpu.SemaphoreType.DMA((16,)),
        ],
        compiler_params=pltpu.CompilerParams(vmem_limit_bytes=VMEM_LIMIT),
        cost_estimate=pl.CostEstimate(flops=2 * 10**9, bytes_accessed=16 * 2**20, transcendentals=2**20),
        name="attention",
    )(bounds, key_doc, query_doc, queries, d_mixed, kv)


def partner_copy(u, src, dst, ss, rs):
    return pltpu.make_async_remote_copy(
        src_ref=src,
        dst_ref=dst,
        send_sem=ss.at[u],
        recv_sem=rs.at[u],
        device_id={"grp": 1 - lax.axis_index("grp")},
        device_id_type=MESH,
    )


def decoder_kernel(
    d_kv, mixed, d_query, dec, cot, w_attn,
    out, grads, kv_grad,
    slots, ring_s, ring_r, out_own, out_send, out_recv, os, orr, stage, arrived, ps, pr,
):
    greet(True)
    ring = Scatter(d_kv, slots, 64, ring_s, ring_r)
    ring.start()
    h = lax.axis_index("head")
    grp = lax.axis_index("grp")

    def out_copy(d):
        return head_copy(d, out_send.at[d - 1], out_recv.at[d - 1], os, orr)

    def columns(owner):
        return pl.ds(pl.multiple_of(owner * 1024, 1024), 1024)

    def half(n, first):
        return pl.ds(pl.multiple_of(first + n * 256, 256), 256)

    for d in (2, 1, 3):
        first = lax.rem(h + d, 4) * 1024
        for n in range(4):
            out_send[d - 1, :, pl.ds(n * 256, 256)] = mm(mixed[...], w_attn[:, half(n, first)]).astype(BF)
        out_copy(d).start()
    ring.step(0)
    for n in range(4):
        here = half(n, h * 1024)
        out_own[:, pl.ds(n * 256, 256)] = mm(mixed[...], w_attn[:, here]) + dec[:, here].astype(F32)

    def products(u):
        t = lax.rem(u + 8 * (1 - grp), 16)
        here = pl.ds(pl.multiple_of(t * 256, 256), 256)
        return mm_rows(dec[:, here], d_query[...]), mm_rows(cot[:, here], mixed[...])

    def exchange(u):
        pair = pl.ds(2 * u, 2)
        return partner_copy(u, stage.at[pair], arrived.at[pair], ps, pr)

    def far(u, c):
        for which, term in enumerate(products(u)):
            for k in range(2):
                stage[2 * u + k, pl.ds(128 * which, 128)] = term[128 * k : 128 * (k + 1)].astype(BF)
        exchange(u).start()
        ring.step(u + 1)
        return c

    lax.fori_loop(0, 8, far, 0)

    def near(u):
        terms = products(u + 8)
        exchange(u).wait_recv()
        for which, term in enumerate(terms):
            for k in range(2):
                rows = pl.ds(128 * which, 128)
                both = term[128 * k : 128 * (k + 1)] + arrived[2 * u + k, rows].astype(F32)
                grads[2 * u + k, rows] = both.astype(BF)

    def near_step(u, c):
        near(u)
        ring.step(u + 9)
        return c

    lax.fori_loop(0, 5, near_step, 0)

    def near_only(u, c):
        near(u)
        return c

    lax.fori_loop(5, 8, near_only, 0)
    total = out_own[...]
    for d in (1, 3, 2):
        out_copy(d).wait_recv()
        total = total + out_recv[d - 1].astype(F32)
    out[...] = total.astype(BF)
    for q in range(4):
        kv_grad[pl.ds(q * 64, 64)] = ring.finish(q).astype(BF)
    ring.drain()
    for d in (1, 2, 3):
        out_copy(d).wait_send()

    def sent(u, c):
        exchange(u).wait_send()
        return c

    lax.fori_loop(0, 8, sent, 0)


def run_decoder(*args):
    sds = jax.ShapeDtypeStruct
    dma = pltpu.SemaphoreType.DMA
    return pl.pallas_call(
        decoder_kernel,
        out_shape=(sds((256, 1024), BF), sds((16, 256, 512), BF), sds((256, 1024), BF)),
        in_specs=[VM] * 6,
        out_specs=(VM,) * 3,
        scratch_shapes=[
            pltpu.VMEM((4, 15, 64, 1024), BF), dma((4, 15)), dma((4, 15)),
            pltpu.VMEM((256, 1024), F32), pltpu.VMEM((3, 256, 1024), BF), pltpu.VMEM((3, 256, 1024), BF),
            dma((3,)), dma((3,)),
            pltpu.VMEM((16, 256, 512), BF), pltpu.VMEM((16, 256, 512), BF), dma((8,)), dma((8,)),
        ],
        compiler_params=pltpu.CompilerParams(
            collective_id=1, has_side_effects=True, vmem_limit_bytes=VMEM_LIMIT
        ),
        cost_estimate=pl.CostEstimate(flops=4 * 10**9, bytes_accessed=24 * 2**20, transcendentals=0),
        name="decoder_scatter",
    )(*args)


def weights_kernel(
    grads, kv_grad, enc_out, normed, pre_act, activated, w_key, w_value, w_out,
    first, second,
    slots1, s1, r1, slots2, s2, r2, parts, slots, d_enc, hs1, hr1, hs2, hr2,
    d_pre, own, stage, arrived, ps, pr,
):
    greet(True)
    grp = lax.axis_index("grp")
    ring = Scatter(grads, slots1, 64, s1, r1)
    ring.start()
    k_grad, v_grad = kv_grad.at[:, pl.ds(0, 512)], kv_grad.at[:, pl.ds(512, 512)]
    for n in range(4):
        rows = pl.ds(n * 256, 256)
        part = mm_cols(k_grad[...], w_key[rows, :]) + mm_cols(v_grad[...], w_value[rows, :])
        parts[:, rows] = part.astype(BF)
    across = HeadSum(parts, slots, d_enc, hs1, hr1, hs2, hr2)
    across.send()
    ring.step(0)
    far, near = (1 - grp) * 512, grp * 512

    def exchange(u):
        places = (pl.ds(0, 64), pl.ds(64, 64), pl.ds(128, 64))
        return partner_copy(u, stage.at[:, places[u]], arrived.at[:, places[u]], ps, pr)

    def term(left, right, row, base):
        for n in range(2):
            cols = pl.ds(pl.multiple_of(base + n * 256, 256), 256)
            value = mm_rows(left[:, cols], right[...])
            for k in range(8):
                yield n * 8 + k, row, value[32 * k : 32 * (k + 1)]

    def put(dst, left, right, row):
        for base, target in ((far, stage), (near, own)):
            for block, place, value in term(left, right, row, base):
                target[block, pl.ds(place, 32)] = value.astype(BF)

    put(None, enc_out, k_grad, 0)
    ring.step(1)
    put(None, enc_out, v_grad, 32)
    exchange(0).start()
    ring.step(2)
    ring.step(3)
    across.share(across.receive())
    ring.step(4)
    ring.step(5)
    ring.step(6)
    across.collect()
    for n in range(4):
        cols = pl.ds(n * 256, 256)
        pre = pre_act[:, cols]
        sig = 1.0 / (1.0 + jnp.exp(-pre))
        slope = sig * (1.0 + pre * (1.0 - sig))
        d_pre[:, cols] = (mm_cols(d_enc[...], w_out[cols, :]) * slope).astype(BF)
    ring.step(7)
    for n in range(2):
        put(None, normed, d_pre.at[:, pl.ds(512 * n, 512)], 64 + 32 * n)
        ring.step(8 + n)
    exchange(1).start()
    for n in range(2):
        put(None, d_enc, activated.at[:, pl.ds(512 * n, 512)], 128 + 32 * n)
        ring.step(10 + n)
    exchange(2).start()
    ring.step(12)
    for u in range(3):
        exchange(u).wait_recv()
    ring.step(13)

    def add(b, c):
        own[b] = (own[b].astype(F32) + arrived[b].astype(F32)).astype(BF)
        return c

    lax.fori_loop(0, 16, add, 0)
    ring2 = Scatter(own, slots2, 48, s2, r2)
    ring2.start()
    for q in range(4):
        first[pl.ds(q * 64, 64)] = ring.finish(q)
    ring.drain()
    across.drain()
    for u in range(3):
        exchange(u).wait_send()

    def body(t, c):
        ring2.step(t)
        return c

    lax.fori_loop(0, 14, body, 0)
    for q in range(4):
        second[pl.ds(q * 48, 48)] = ring2.finish(q)
    ring2.drain()


def run_weights(*args):
    sds = jax.ShapeDtypeStruct
    dma = pltpu.SemaphoreType.DMA
    return pl.pallas_call(
        weights_kernel,
        out_shape=(sds((256, 512), F32), sds((192, 512), F32)),
        in_specs=[VM] * 9,
        out_specs=(VM,) * 2,
        scratch_shapes=[
            pltpu.VMEM((4, 15, 64, 512), BF), dma((4, 15)), dma((4, 15)),
            pltpu.VMEM((4, 15, 48, 512), BF), dma((4, 15)), dma((4, 15)),
            pltpu.VMEM((256, 1024), BF), pltpu.VMEM((3, 64, 1024), BF), pltpu.VMEM((256, 1024), BF),
            dma((3,)), dma((3,)), dma((3,)), dma((3,)),
            pltpu.VMEM((256, 1024), BF),
            pltpu.VMEM((16, 192, 512), BF), pltpu.VMEM((16, 192, 512), BF), pltpu.VMEM((16, 192, 512), BF),
            dma((3,)), dma((3,)),
        ],
        compiler_params=pltpu.CompilerParams(
            collective_id=2, has_side_effects=True, vmem_limit_bytes=VMEM_LIMIT
        ),
        cost_estimate=pl.CostEstimate(flops=3 * 10**9, bytes_accessed=16 * 2**20, transcendentals=2**18),
        name="weights_scatter",
    )(*args)


def shards(
    enc_in, enc_gain, w_in, w_out, w_key, w_value, dec_in, w_query, w_attn_out, cotangent, group_doc, doc_lengths,
):
    positions = lax.axis_index("seq") * 256 + jnp.arange(256, dtype=jnp.int32)
    earlier = jnp.arange(8)[:, None] <= jnp.arange(8)[None, :]
    doc_ends = jnp.sum(jnp.where(earlier, doc_lengths[0][:, None], 0), axis=0)
    query_doc = jnp.sum((positions[:, None] >= doc_ends[None, :]).astype(jnp.int32), axis=1)
    key_doc = group_doc[0]
    lo = jnp.sum((key_doc < query_doc[0]).astype(jnp.int32))
    hi = jnp.sum((key_doc <= query_doc[255]).astype(jnp.int32))
    bounds = jnp.stack([lo, hi])
    normed, pre_act, activated, enc_out, kv, queries, d_mixed = run_encoder(
        enc_in[0], enc_gain[None, :], w_in, w_out, w_key, w_value, dec_in[0], w_query, w_attn_out, cotangent[0]
    )
    mixed, d_query, d_kv = run_attention(bounds, key_doc, query_doc[:, None], queries, d_mixed, kv)
    out, grads, kv_grad = run_decoder(d_kv, mixed, d_query, dec_in[0], cotangent[0], w_attn_out)
    first, second = run_weights(
        grads, kv_grad, enc_out, normed, pre_act, activated, w_key, w_value, w_out
    )
    g_query, g_attn = first[:128], first[128:].T
    g_key, g_value = second[:32], second[32:64]
    g_in = jnp.concatenate([second[64:96], second[96:128]], axis=1)
    g_out = jnp.concatenate([second[128:160], second[160:192]], axis=1).T
    return (out[None], g_query, g_key, g_value, g_attn, g_in, g_out)


def solution(mesh):
    placed = (
        P("grp", "seq", None),
        P(),
        P(None, "head"),
        P("head", None),
        P(None, "head"),
        P(None, "head"),
        P("grp", "seq", None),
        P(None, "head"),
        P("head", None),
        P("grp", "seq", None),
        P("grp", None),
        P("grp", None),
    )
    return jax.shard_map(
        shards,
        mesh=mesh,
        in_specs=placed,
        out_specs=(
            P("grp", "seq", "head"),
            P(("grp", "seq"), "head"),
            P(("grp", "seq"), "head"),
            P(("grp", "seq"), "head"),
            P("head", ("grp", "seq")),
            P(("grp", "seq"), "head"),
            P("head", ("grp", "seq")),
        ),
        check_vma=False,
    )
```

time: 951 us -> 359 us (0.38)
  waiting for transfers between devices: 754 us -> 0 us
  Pallas kernels: 0 us -> 346 us
  matrix products: 84.1 us -> 0 us
  local copies, waits for them, and re-layouts: 40.2 us -> 6.47 us
  blocking collectives: 33.2 us -> 0 us
  other arithmetic: 22.1 us -> 6.01 us
  between operations: 14.4 us -> 0.68 us
    reduce_scatter x7 -> x0, waiting for transfers between devices: 492 us -> none  [the longest x1 80.4 us: shards(): lax.psum_scatter(inner_rows(normed, d_pre).astype(jnp.bfloat16), ('grp',...]
    pallas_call x0 -> x4, Pallas kernels: none -> 346 us  [the longest x1 122 us: run_weights(): pl.pallas_call(weights_kernel, out_shape=(sds((256, 512), F32), sds((192,...]
    unnamed x14 -> x0, waiting for transfers between devices: 121 us -> none
    all_gather x2 -> x0, waiting for transfers between devices: 92.2 us -> none  [the longest x1 48.7 us: shards(): lax.all_gather(keys_own, 'seq', axis=0, tiled=True)]
    dot_general x39 -> x0, matrix products: 84.1 us -> none  [the longest x14 31.6 us: matmul(): return jnp.dot(left_side, right_side, preferred_element_type=jnp.float32)]
    psum x1 -> x0, waiting for transfers between devices: 48.3 us -> none  [shards(): summed = lax.psum(matmul(activated, w_out), 'head')]
    psum x1 -> x0, blocking collectives: 33.2 us -> none  [shards(): lax.psum(inner_cols(key_grad, w_key) + inner_cols(value_grad, w_value), '...]
    unnamed x31 -> x4, local copies, waits for them, and re-layouts: 17.4 us -> 1.63 us
  transfers between devices with their start and end apart: 12 -> 0, of which waited for: 12 -> 0; matrix products, arithmetic and copies ran while one was open for 7% -> 0% of each run, Pallas kernels for 0% -> 0%
where the time goes in v1:
time: 359 us
  Pallas kernels  346 us (96%)
  local copies, waits for them, and re-layouts  6.47 us (2%)
  other arithmetic  6.01 us (2%)
    pallas_call x1, Pallas kernels, run_weights(): pl.pallas_call(weights_kernel, out_shape=(sds((256, 512), F32), sds((192,...  122 us
    pallas_call x1, Pallas kernels, run_decoder(): pl.pallas_call(decoder_kernel, out_shape=(sds((256, 1024), BF), sds((16,...  108 us
    pallas_call x1, Pallas kernels, run_encoder(): pl.pallas_call(encoder_kernel, out_shape=(sds((256, 1024), BF), sds((256,...  102 us
    pallas_call x1, Pallas kernels, run_attention(): pl.pallas_call(attention_kernel, out_shape=(sds((256, 512), BF), sds((256...  14.2 us

profile of v1, /device:TPU:0, one launch (start us, length us, event | category | flops | bytes accessed | tf_op | source)
XLA Modules:
  0.0 359.2 jit_solution(5824490351709399284)
XLA Ops:
  0.6 0.7 select_reduce_fusion
  1.4 0.1 convert_reduce_fusion
  1.5 0.6 fusion.3
  2.1 2.6 fusion
  4.6 1.9 pad_add_fusion.bounds
  6.5 0.8 copy.22.query_doc
  7.3 102.1 %encoder_gather.1 = (bf16[256,1024]{1,0:T(8,128)(2,1)}, f32[256,1024]{1,0:T(8,128)}, bf16[256,1024]{1,0:T(8,128)(2,1)}, bf16[256,1024]{1,0:T(8,128)(2,1)}, bf16[...) custom-call(bf16[256,1024]{1,0:T(8,128)(2,1)} %bitcast.23, f32[1,1024]{1,0:T(1,128)} %bitcast.25, ...), custom_call_target="tpu_custom_call" | custom-call | flops 5000000000 | bytes 31457280 | tf_op jit(solution)/shard_map/encoder_gather/pallas_call | solution.py:301
  109.5 14.2 %attention.1 = (bf16[256,512]{1,0:T(8,128)(2,1)}, bf16[256,512]{1,0:T(8,128)(2,1)}, bf16[16,256,1024]{2,1,0:T(8,128)(2,1)}) custom-call(s32[2]{0:T(128)} %pad_add_fusion.bounds, s32[16]{0:T(128)} %bitcast.26, s32[256,1]{1,0:T(8,128)} %copy.22.query_doc, bf16[256,512]{1,0:T(8,128)(2,1)} %get-tuple-element.22.queries, ...), custom_call_target="tpu_custom_call" | custom-call | flops 2000000000 | bytes 16777216 | tf_op jit(solution)/shard_map/attention/pallas_call | solution.py:396
  123.7 108.0 %decoder_scatter.1 = (bf16[256,1024]{1,0:T(8,128)(2,1)}, bf16[16,256,512]{2,1,0:T(8,128)(2,1)}, bf16[256,1024]{1,0:T(8,128)(2,1)}) custom-call(bf16[16,256,1024]{2,1,0:T(8,128)(2,1)} %get-tuple-element.25.d_kv, bf16[256,512]{1,0:T(8,128)(2,1)} %get-tuple-element.26.mixed, bf16[256,512]{1,0:T(8,128)(2,1)} %get-tuple-element.27.d_query, ...), custom_call_target="tpu_custom_call" | custom-call | flops 4000000000 | bytes 25165824 | tf_op jit(solution)/shard_map/decoder_scatter/pallas_call | solution.py:513
  231.7 0.0 copy-start
  231.7 121.6 %weights_scatter.1 = (f32[256,512]{1,0:T(8,128)}, f32[192,512]{1,0:T(8,128)}) custom-call(bf16[16,256,512]{2,1,0:T(8,128)(2,1)} %get-tuple-element.29.grads, bf16[256,1024]{1,0:T(8,128)(2,1)} %get-tuple-element.30.kv_grad, bf16[256,1024]{1,0:T(8,128)(2,1)} %get-tuple-element.31.enc_out, bf16[256,1024]{1,0:T(8,128)(2,1)} %get-tuple-element.32.normed, ...), custom_call_target="tpu_custom_call" | custom-call | flops 3000000000 | bytes 16777216 | tf_op jit(solution)/shard_map/weights_scatter/pallas_call | solution.py:626
  353.4 1.8 slice_bitcast_fusion
  355.2 0.8 copy.23
  356.0 1.7 fusion.2
  357.7 0.7 pad_maximum_fusion
  358.4 0.0 copy-done
  358.4 0.8 copy.25
  (1 shorter events, 0.0 us)
Async XLA Ops:
  231.7 126.7 %copy-start = (bf16[256,1024]{1,0:T(8,128)(2,1)S(1)}, bf16[256,1024]{1,0:T(8,128)(2,1)}, u32[]{:S(2)}) copy-start(bf16[256,1024]{1,0:T(8,128)(2,1)} %get-tuple-element.28) | copy-start | bytes 1572868

commit v2 on v1

v2 whole, which is shorter than its diff:
```python
import functools
import math

import jax
import jax.numpy as jnp
from jax import lax
from jax.experimental import pallas as pl
from jax.experimental.pallas import tpu as pltpu
from jax.sharding import PartitionSpec as P

HEAD_DIM = 128
GROUP = 256
N_SEQ = 16
N_HEAD = 4
EPSILON = 1e-06
MASKED = -1e30
SCALE = 1.0 / math.sqrt(HEAD_DIM)
MESH = pl.DeviceIdType.MESH
BF = jnp.bfloat16
F32 = jnp.float32
VMEM_LIMIT = 62 * 1024 * 1024
VM = pl.BlockSpec(memory_space=pltpu.VMEM)
ANY = pl.BlockSpec(memory_space=pl.ANY)


def mm(a, b):
    return lax.dot_general(a, b, (((1,), (0,)), ((), ())), preferred_element_type=F32)


def mm_rows(a, b):
    return lax.dot_general(a, b, (((0,), (0,)), ((), ())), preferred_element_type=F32)


def mm_cols(a, b):
    return lax.dot_general(a, b, (((1,), (1,)), ((), ())), preferred_element_type=F32)


def place():
    s = lax.axis_index("seq")
    return s >> 2, s & 3


def x_copy(d, src, dst, send_sem, recv_sem):
    z, x = place()
    return pltpu.make_async_remote_copy(
        src_ref=src,
        dst_ref=dst,
        send_sem=send_sem,
        recv_sem=recv_sem,
        device_id={"seq": 4 * z + ((x + d) & 3)},
        device_id_type=MESH,
    )


def z_copy(d, src, dst, send_sem, recv_sem):
    z, x = place()
    return pltpu.make_async_remote_copy(
        src_ref=src,
        dst_ref=dst,
        send_sem=send_sem,
        recv_sem=recv_sem,
        device_id={"seq": 4 * ((z + d) & 3) + x},
        device_id_type=MESH,
    )


def greet(with_partner):
    z, x = place()
    h = lax.axis_index("head")
    barrier = pltpu.get_barrier_semaphore()
    for d in range(1, 4):
        for peer in (
            {"seq": 4 * z + ((x + d) & 3)},
            {"seq": 4 * ((z + d) & 3) + x},
            {"head": (h + d) & 3},
        ):
            pl.semaphore_signal(barrier, inc=1, device_id=peer, device_id_type=MESH)
    if with_partner:
        pl.semaphore_signal(
            barrier, inc=1, device_id={"grp": 1 - lax.axis_index("grp")}, device_id_type=MESH
        )


def met(with_partner):
    pl.semaphore_wait(pltpu.get_barrier_semaphore(), 10 if with_partner else 9)


def partner_copy(src, dst, send_sem, recv_sem):
    return pltpu.make_async_remote_copy(
        src_ref=src,
        dst_ref=dst,
        send_sem=send_sem,
        recv_sem=recv_sem,
        device_id={"grp": 1 - lax.axis_index("grp")},
        device_id_type=MESH,
    )


class Swap:
    def __init__(self, source, target, ss, rs):
        self.source, self.target, self.ss, self.rs = source, target, ss, rs
        self.x = place()[1]

    def sending(self, d):
        src = self.source.at[(self.x + d) & 3]
        return x_copy(d, src, self.target.at[self.x], self.ss.at[d - 1], self.rs.at[d - 1])

    def landing(self, d):
        ref = self.target.at[(self.x + 4 - d) & 3]
        return x_copy(d, ref, ref, self.ss.at[d - 1], self.rs.at[d - 1])

    def start(self):
        for d in (2, 1, 3):
            self.sending(d).start()

    def keep(self):
        self.target[self.x] = self.source[self.x]

    def finish(self):
        for d in (1, 3, 2):
            self.landing(d).wait_recv()

    def drain(self):
        for d in (1, 2, 3):
            self.sending(d).wait_send()


class Scatter:
    def __init__(self, blocks, n, slots, sums, last, ss, rs, ss2, rs2):
        self.blocks, self.n = blocks, n
        self.slots, self.sums, self.last = slots, sums, last
        self.ss, self.rs, self.ss2, self.rs2 = ss, rs, ss2, rs2
        self.z, self.x = place()

    def cut(self, half, d):
        rows = pl.ds(half * self.n, self.n)
        if half == 0:
            return self.blocks.at[:, (self.x + d) & 3, rows]
        return self.blocks.at[(self.z + d) & 3, :, rows]

    def first(self, half, d):
        move = x_copy if half == 0 else z_copy
        return move(
            d, self.cut(half, d), self.slots.at[half, d - 1], self.ss.at[half, d - 1], self.rs.at[half, d - 1]
        )

    def second(self, half, d):
        move = z_copy if half == 0 else x_copy
        own = self.z if half == 0 else self.x
        return move(
            d, self.sums.at[half, (own + d) & 3], self.last.at[half, d - 1],
            self.ss2.at[half, d - 1], self.rs2.at[half, d - 1],
        )

    def start(self):
        for d in (2, 1, 3):
            for half in (0, 1):
                self.first(half, d).start()

    def middle(self):
        for half in (0, 1):
            for d in (1, 3, 2):
                self.first(half, d).wait_recv()
            own = self.cut(half, 0)

            def add(k, c):
                total = own[k].astype(F32) + self.slots[half, 0, k].astype(F32)
                total = total + self.slots[half, 1, k].astype(F32) + self.slots[half, 2, k].astype(F32)
                self.sums[half, k] = total.astype(BF)
                return c

            lax.fori_loop(0, 4, add, 0)
            for d in (2, 1, 3):
                self.second(half, d).start()

    def finish(self, half):
        for d in (1, 3, 2):
            self.second(half, d).wait_recv()
        own = self.z if half == 0 else self.x
        total = self.sums[half, own].astype(F32)
        for d in range(3):
            total = total + self.last[half, d].astype(F32)
        return total

    def drain(self):
        for half in (0, 1):
            for d in (1, 2, 3):
                self.first(half, d).wait_send()
                self.second(half, d).wait_send()

    @staticmethod
    def scratch(n):
        dma = pltpu.SemaphoreType.DMA
        return [
            pltpu.VMEM((2, 3, 4, n, 512), BF), pltpu.VMEM((2, 4, n, 512), BF), pltpu.VMEM((2, 3, n, 512), BF),
            dma((2, 3)), dma((2, 3)), dma((2, 3)), dma((2, 3)),
        ]


def head_copy(d, src, dst, ss, rs):
    h = lax.axis_index("head")
    return pltpu.make_async_remote_copy(
        src_ref=src,
        dst_ref=dst,
        send_sem=ss.at[d - 1],
        recv_sem=rs.at[d - 1],
        device_id={"head": lax.rem(h + d, 4)},
        device_id_type=MESH,
    )


class HeadSum:
    def __init__(self, parts, slots, total, ss, rs, ss2, rs2):
        self.parts, self.slots, self.total = parts, slots, total
        self.ss, self.rs, self.ss2, self.rs2 = ss, rs, ss2, rs2
        self.h = lax.axis_index("head")

    def quarter(self, h):
        return pl.ds(pl.multiple_of(h * 64, 64), 64)

    def first(self, d):
        src = self.parts.at[self.quarter(lax.rem(self.h + d, 4))]
        return head_copy(d, src, self.slots.at[d - 1], self.ss, self.rs)

    def second(self, d):
        ref = self.total.at[self.quarter(self.h)]
        return head_copy(d, ref, ref, self.ss2, self.rs2)

    def second_landing(self, d):
        ref = self.total.at[self.quarter(lax.rem(self.h + 4 - d, 4))]
        return head_copy(d, ref, ref, self.ss2, self.rs2)

    def send(self):
        for d in (2, 1, 3):
            self.first(d).start()

    def receive(self):
        total = self.parts[self.quarter(self.h)].astype(F32)
        for d in (1, 3, 2):
            self.first(d).wait_recv()
            total = total + self.slots[d - 1].astype(F32)
        return total

    def share(self, total):
        self.total[self.quarter(self.h)] = total.astype(BF)
        for d in (2, 1, 3):
            self.second(d).start()

    def collect(self):
        for d in (1, 3, 2):
            self.second_landing(d).wait_recv()

    def drain(self):
        for d in (1, 2, 3):
            self.first(d).wait_send()
            self.second(d).wait_send()


def encoder_kernel(
    enc_in, gain, w_in, w_out, w_key, w_value, dec, w_query, w_attn, cot,
    normed, pre_act, activated, enc_out, kv, q_all, dm_all,
    v_in, v_out, v_key, v_value, v_dec, v_query, v_attn, v_cot, load_sem,
    parts, slots, hs1, hr1, hs2, hr2,
    q_send, dm_send, kv_send, qs, qr, ds, dr, ks, kr, zs, zr,
):
    pairs = (
        (w_in, v_in), (w_out, v_out), (dec, v_dec), (w_query, v_query),
        (w_key, v_key), (w_value, v_value), (cot, v_cot), (w_attn, v_attn),
    )
    loads = {id(v): pltpu.make_async_copy(a, v, load_sem.at[i]) for i, (a, v) in enumerate(pairs)}
    greet(False)
    for copy in loads.values():
        copy.start()
    z, x = place()
    encoded = enc_in[...].astype(F32)
    square = jnp.mean(encoded * encoded, axis=1, keepdims=True)
    normed[...] = (encoded * lax.rsqrt(square + EPSILON) * gain[...]).astype(BF)
    loads[id(v_in)].wait()
    for n in range(4):
        cols = pl.ds(n * 256, 256)
        pre = mm(normed[...], v_in[:, cols])
        pre_act[:, cols] = pre
        activated[:, cols] = (pre / (1.0 + jnp.exp(-pre))).astype(BF)
    loads[id(v_out)].wait()
    for n in range(4):
        cols = pl.ds(n * 256, 256)
        parts[:, cols] = mm(activated[...], v_out[:, cols]).astype(BF)
    met(False)
    across = HeadSum(parts, slots, enc_out, hs1, hr1, hs2, hr2)
    across.send()
    q_swap = Swap(q_send, q_all, qs, qr)
    dm_swap = Swap(dm_send, dm_all, ds, dr)
    kv_swap = Swap(kv_send, kv.at[pl.ds(4 * z, 4)], ks, kr)
    loads[id(v_dec)].wait()
    loads[id(v_query)].wait()
    for n in range(2):
        rows = mm(v_dec[...], v_query[:, pl.ds(n * 256, 256)]).astype(BF)
        q_send[2 * n], q_send[2 * n + 1] = rows[:, :128], rows[:, 128:]
    q_swap.start()
    own_rows = across.quarter(across.h)
    across.share(across.receive() + enc_in[own_rows].astype(F32))
    loads[id(v_cot)].wait()
    loads[id(v_attn)].wait()
    for n in range(2):
        rows = mm_cols(v_cot[...], v_attn[pl.ds(n * 256, 256), :]).astype(BF)
        dm_send[2 * n], dm_send[2 * n + 1] = rows[:, :128], rows[:, 128:]
    loads[id(v_key)].wait()
    loads[id(v_value)].wait()
    across.collect()
    for n in range(2):
        for weight, first in ((v_key, 0), (v_value, 128)):
            rows = mm(enc_out[...], weight[:, pl.ds(n * 256, 256)]).astype(BF)
            kv_send[2 * n, :, pl.ds(first, 128)] = rows[:, :128]
            kv_send[2 * n + 1, :, pl.ds(first, 128)] = rows[:, 128:]
    kv_swap.start()
    kv_swap.keep()

    def forward(k, d):
        ref = kv.at[4 * z + ((x + k) & 3)]
        return z_copy(d, ref, ref, zs.at[d - 1, k], zr.at[d - 1, k])

    def arriving(k, d):
        ref = kv.at[4 * ((z + 4 - d) & 3) + ((x + k) & 3)]
        return z_copy(d, ref, ref, zs.at[d - 1, k], zr.at[d - 1, k])

    for d in (2, 1, 3):
        forward(0, d).start()
    dm_swap.start()
    for k in (3, 1, 2):
        kv_swap.landing(4 - k).wait_recv()
        for d in (2, 1, 3):
            forward(k, d).start()
    q_swap.keep()
    dm_swap.keep()
    q_swap.finish()
    dm_swap.finish()
    for k in (0, 3, 1, 2):
        for d in (1, 3, 2):
            arriving(k, d).wait_recv()
    for k in range(4):
        for d in (1, 2, 3):
            forward(k, d).wait_send()
    for swap in (q_swap, dm_swap, kv_swap):
        swap.drain()
    across.drain()


def run_encoder(*args):
    sds = jax.ShapeDtypeStruct
    dma = pltpu.SemaphoreType.DMA
    return pl.pallas_call(
        encoder_kernel,
        out_shape=(
            sds((256, 1024), BF), sds((256, 1024), F32), sds((256, 1024), BF), sds((256, 1024), BF),
            sds((16, 256, 256), BF), sds((4, 256, 128), BF), sds((4, 256, 128), BF),
        ),
        in_specs=[VM, VM] + [ANY] * 8,
        out_specs=(VM,) * 7,
        scratch_shapes=[
            pltpu.VMEM((1024, 1024), BF), pltpu.VMEM((1024, 1024), BF),
            pltpu.VMEM((1024, 512), BF), pltpu.VMEM((1024, 512), BF),
            pltpu.VMEM((256, 4096), BF), pltpu.VMEM((4096, 512), BF),
            pltpu.VMEM((512, 4096), BF), pltpu.VMEM((256, 4096), BF), dma((8,)),
            pltpu.VMEM((256, 1024), BF), pltpu.VMEM((3, 64, 1024), BF),
            dma((3,)), dma((3,)), dma((3,)), dma((3,)),
            pltpu.VMEM((4, 256, 128), BF), pltpu.VMEM((4, 256, 128), BF), pltpu.VMEM((4, 256, 256), BF),
            dma((3,)), dma((3,)), dma((3,)), dma((3,)), dma((3,)), dma((3,)), dma((3, 4)), dma((3, 4)),
        ],
        compiler_params=pltpu.CompilerParams(
            collective_id=0, has_side_effects=True, vmem_limit_bytes=VMEM_LIMIT
        ),
        cost_estimate=pl.CostEstimate(flops=5 * 10**9, bytes_accessed=24 * 2**20, transcendentals=2**18),
        name="encoder_gather",
    )(*args)


def attention_kernel(group_doc, doc_lengths, q_all, dm_all, kv, md, d_kv, scores, acc, d_acc, ends, begins, limits):
    z = lax.axis_index("seq") >> 2
    total = 0
    for j in range(8):
        total = total + doc_lengths[0, j]
        ends[j] = total
    for g in range(N_SEQ):
        doc = group_doc[0, g]
        limits[g] = ends[doc]
        begins[g] = ends[doc] - doc_lengths[0, doc]
    bounds = []
    for b in range(4):
        origin = z * 1024 + b * 256
        lo, hi = 0, 0
        for g in range(N_SEQ):
            lo = lo + jnp.where(limits[g] <= origin, 1, 0)
            hi = hi + jnp.where(begins[g] <= origin + 255, 1, 0)
        bounds.append((origin, lo, hi))
    low, high = bounds[0][1], bounds[3][2]

    def clear(g, c):
        inside = (g >= low) & (g < high)

        @pl.when(inside)
        def _():
            d_acc[g] = jnp.zeros((256, 256), F32)

        @pl.when(jnp.logical_not(inside))
        def _():
            d_kv[g] = jnp.zeros((256, 256), BF)

        return c

    lax.fori_loop(0, N_SEQ, clear, 0)
    for b in range(4):
        origin, lo, hi = bounds[b]
        position = origin + lax.broadcasted_iota(jnp.int32, (256, 1), 0)

        def score(g, m):
            s = mm_cols(q_all[b], kv[g, :, pl.ds(0, 128)]) * SCALE
            seen = (position >= begins[g]) & (position < limits[g])
            s = jnp.where(seen, s, MASKED)
            scores[g] = s
            return jnp.maximum(m, jnp.max(s, axis=1, keepdims=True))

        top = lax.fori_loop(lo, hi, score, jnp.full((256, 1), MASKED, F32))
        acc[...] = jnp.zeros((256, 128), F32)

        def weigh(g, total):
            p = jnp.exp(scores[g] - top)
            scores[g] = p
            acc[...] += mm(p.astype(BF), kv[g, :, pl.ds(128, 128)])
            return total + jnp.sum(p, axis=1, keepdims=True)

        total = lax.fori_loop(lo, hi, weigh, jnp.zeros((256, 1), F32))
        inverse = 1.0 / total
        rows = acc[...] * inverse
        md[b, :, pl.ds(0, 128)] = rows.astype(BF)
        inner = jnp.sum(rows * dm_all[b].astype(F32), axis=1, keepdims=True)
        acc[...] = jnp.zeros((256, 128), F32)

        def back(g, c):
            p = scores[g] * inverse
            dw = mm_cols(dm_all[b], kv[g, :, pl.ds(128, 128)])
            ds = (p * (dw - inner) * SCALE).astype(BF)
            acc[...] += mm(ds, kv[g, :, pl.ds(0, 128)])
            d_acc[g, :, pl.ds(0, 128)] += mm_rows(ds, q_all[b])
            d_acc[g, :, pl.ds(128, 128)] += mm_rows(p.astype(BF), dm_all[b])
            return c

        lax.fori_loop(lo, hi, back, 0)
        md[b, :, pl.ds(128, 128)] = acc[...].astype(BF)

    def settle(g, c):
        d_kv[g] = d_acc[g].astype(BF)
        return c

    lax.fori_loop(low, high, settle, 0)


def run_attention(*args):
    sds = jax.ShapeDtypeStruct
    smem = pl.BlockSpec(memory_space=pltpu.SMEM)
    return pl.pallas_call(
        attention_kernel,
        out_shape=(sds((4, 256, 256), BF), sds((16, 256, 256), BF)),
        in_specs=[smem, smem, VM, VM, VM],
        out_specs=(VM,) * 2,
        scratch_shapes=[
            pltpu.VMEM((16, 256, 256), F32), pltpu.VMEM((256, 128), F32), pltpu.VMEM((16, 256, 256), F32),
            pltpu.SMEM((8,), jnp.int32), pltpu.SMEM((16,), jnp.int32), pltpu.SMEM((16,), jnp.int32),
        ],
        compiler_params=pltpu.CompilerParams(vmem_limit_bytes=VMEM_LIMIT),
        cost_estimate=pl.CostEstimate(flops=2 * 10**9, bytes_accessed=6 * 2**20, transcendentals=2**20),
        name="attention",
    )(*args)


def decoder_kernel(
    d_kv, md, dec, cot, w_attn,
    out, grads, kv_grad,
    v_dec, v_cot, v_attn, load_sem,
    m_all, ms, mr, row_slots, zs, zr, row, kvg, ks, kr, mixed, d_query,
    out_own, out_send, out_recv, os, orr, stage, arrived, ps, pr,
):
    greet(True)
    loads = [
        pltpu.make_async_copy(a, v, load_sem.at[i])
        for i, (a, v) in enumerate(((w_attn, v_attn), (dec, v_dec), (cot, v_cot)))
    ]
    for load in loads:
        load.start()
    met(True)
    z, x = place()
    h = lax.axis_index("head")
    grp = lax.axis_index("grp")
    m_swap = Swap(md, m_all, ms, mr)
    kv_swap = Swap(row, kvg, ks, kr)

    def term(k, d):
        src = d_kv.at[4 * ((z + d) & 3) + ((x + k) & 3)]
        return z_copy(d, src, row_slots.at[d - 1, k], zs.at[d - 1, k], zr.at[d - 1, k])

    m_swap.start()
    for k in (2, 1, 3, 0):
        for d in (2, 1, 3):
            term(k, d).start()
    m_swap.keep()
    m_swap.finish()
    for j in range(4):
        mixed[:, pl.ds(128 * j, 128)] = m_all[j, :, pl.ds(0, 128)]
        d_query[:, pl.ds(128 * j, 128)] = m_all[j, :, pl.ds(128, 128)]

    def out_copy(d):
        return head_copy(d, out_send.at[d - 1], out_recv.at[d - 1], os, orr)

    def part(n, first):
        return pl.ds(pl.multiple_of(first + n * 256, 256), 256)

    loads[0].wait()
    for d in (2, 1, 3):
        first = ((h + d) & 3) * 1024
        for n in range(4):
            out_send[d - 1, :, pl.ds(n * 256, 256)] = mm(mixed[...], v_attn[:, part(n, first)]).astype(BF)
        out_copy(d).start()
    loads[1].wait()
    loads[2].wait()

    def products(u):
        t = (u + 8 * (1 - grp)) & 15
        here = pl.ds(pl.multiple_of(t * 256, 256), 256)
        return mm_rows(v_dec[:, here], d_query[...]), mm_rows(v_cot[:, here], mixed[...])

    def exchange(u):
        pair = pl.ds(2 * u, 2)
        return partner_copy(stage.at[pair], arrived.at[pair], ps.at[u], pr.at[u])

    def far(u, c):
        for which, value in enumerate(products(u)):
            for k in range(2):
                stage[2 * u + k, pl.ds(128 * which, 128)] = value[128 * k : 128 * (k + 1)].astype(BF)
        exchange(u).start()
        return c

    lax.fori_loop(0, 8, far, 0)

    for n in range(4):
        here = part(n, h * 1024)
        out_own[:, pl.ds(n * 256, 256)] = mm(mixed[...], v_attn[:, here]) + v_dec[:, here].astype(F32)

    def near(u, c):
        values = products(u + 8)
        exchange(u).wait_recv()
        for which, value in enumerate(values):
            for k in range(2):
                rows = pl.ds(128 * which, 128)
                both = value[128 * k : 128 * (k + 1)] + arrived[2 * u + k, rows].astype(F32)
                grads[2 * u + k, rows] = both.astype(BF)
        return c

    lax.fori_loop(0, 8, near, 0)

    for k in (2, 1, 3, 0):
        there = (x + k) & 3
        total = d_kv[4 * z + there].astype(F32)
        for d in (1, 3, 2):
            term(k, d).wait_recv()
            total = total + row_slots[d - 1, k].astype(F32)
        row[there] = total.astype(BF)
        if k:
            kv_swap.sending(k).start()
    kv_swap.keep()
    total = out_own[...]
    for d in (1, 3, 2):
        out_copy(d).wait_recv()
        total = total + out_recv[d - 1].astype(F32)
    out[...] = total.astype(BF)
    kv_swap.finish()
    for j in range(4):
        kv_grad[:, pl.ds(128 * j, 128)] = kvg[j, :, pl.ds(0, 128)]
        kv_grad[:, pl.ds(512 + 128 * j, 128)] = kvg[j, :, pl.ds(128, 128)]
    m_swap.drain()
    kv_swap.drain()
    for k in range(4):
        for d in (1, 2, 3):
            term(k, d).wait_send()
    for d in (1, 2, 3):
        out_copy(d).wait_send()

    def sent(u, c):
        exchange(u).wait_send()
        return c

    lax.fori_loop(0, 8, sent, 0)


def run_decoder(*args):
    sds = jax.ShapeDtypeStruct
    dma = pltpu.SemaphoreType.DMA
    return pl.pallas_call(
        decoder_kernel,
        out_shape=(sds((256, 1024), BF), sds((16, 256, 512), BF), sds((256, 1024), BF)),
        in_specs=[VM, VM, ANY, ANY, ANY],
        out_specs=(VM,) * 3,
        scratch_shapes=[
            pltpu.VMEM((256, 4096), BF), pltpu.VMEM((256, 4096), BF), pltpu.VMEM((512, 4096), BF), dma((3,)),
            pltpu.VMEM((4, 256, 256), BF), dma((3,)), dma((3,)),
            pltpu.VMEM((3, 4, 256, 256), BF), dma((3, 4)), dma((3, 4)),
            pltpu.VMEM((4, 256, 256), BF), pltpu.VMEM((4, 256, 256), BF), dma((3,)), dma((3,)),
            pltpu.VMEM((256, 512), BF), pltpu.VMEM((256, 512), BF),
            pltpu.VMEM((256, 1024), F32), pltpu.VMEM((3, 256, 1024), BF), pltpu.VMEM((3, 256, 1024), BF),
            dma((3,)), dma((3,)),
            pltpu.VMEM((16, 256, 512), BF), pltpu.VMEM((16, 256, 512), BF), dma((8,)), dma((8,)),
        ],
        compiler_params=pltpu.CompilerParams(
            collective_id=1, has_side_effects=True, vmem_limit_bytes=VMEM_LIMIT
        ),
        cost_estimate=pl.CostEstimate(flops=4 * 10**9, bytes_accessed=20 * 2**20, transcendentals=0),
        name="decoder_scatter",
    )(*args)


def weights_kernel(
    grads, kv_grad, enc_out, normed, pre_act, activated, w_key, w_value, w_out,
    first, second,
    *scratch,
):
    ring_a, ring_b, ring_c = scratch[0:7], scratch[7:14], scratch[14:21]
    (
        parts, slots, d_enc, hs1, hr1, hs2, hr2, d_pre,
        own_b, stage_b, arrived_b, own_c, stage_c, arrived_c, ps, pr,
    ) = scratch[21:]
    greet(True)
    grp = lax.axis_index("grp")
    k_grad, v_grad = kv_grad.at[:, pl.ds(0, 512)], kv_grad.at[:, pl.ds(512, 512)]
    for n in range(4):
        rows = pl.ds(n * 256, 256)
        part = mm_cols(k_grad[...], w_key[rows, :]) + mm_cols(v_grad[...], w_value[rows, :])
        parts[:, rows] = part.astype(BF)
    met(True)
    across = HeadSum(parts, slots, d_enc, hs1, hr1, hs2, hr2)
    across.send()
    scatter_a = Scatter(grads, 128, *ring_a)
    scatter_a.start()
    far, near = (1 - grp) * 512, grp * 512

    def put(left, right, row, stage, own):
        for base, target in ((far, stage), (near, own)):
            for n in range(2):
                cols = pl.ds(pl.multiple_of(base + n * 256, 256), 256)
                value = mm_rows(left[:, cols], right[...])
                for k in range(8):
                    block = n * 8 + k
                    target[block // 4, block % 4, pl.ds(row, 32)] = value[32 * k : 32 * (k + 1)].astype(BF)

    def add(own, arrived):
        def body(b, c):
            own[b] = (own[b].astype(F32) + arrived[b].astype(F32)).astype(BF)
            return c

        lax.fori_loop(0, 4, body, 0)

    swap_b = partner_copy(stage_b, arrived_b, ps.at[0], pr.at[0])
    put(enc_out, k_grad, 0, stage_b, own_b)
    put(enc_out, v_grad, 32, stage_b, own_b)
    swap_b.start()
    across.share(across.receive())
    swap_b.wait_recv()
    add(own_b, arrived_b)
    scatter_b = Scatter(own_b, 32, *ring_b)
    scatter_b.start()
    across.collect()
    for n in range(4):
        cols = pl.ds(n * 256, 256)
        pre = pre_act[:, cols]
        sig = 1.0 / (1.0 + jnp.exp(-pre))
        slope = sig * (1.0 + pre * (1.0 - sig))
        d_pre[:, cols] = (mm_cols(d_enc[...], w_out[cols, :]) * slope).astype(BF)
    halves = [pl.ds(64 * which, 64) for which in range(2)]
    swap_c = [
        partner_copy(stage_c.at[:, :, r], arrived_c.at[:, :, r], ps.at[1 + i], pr.at[1 + i])
        for i, r in enumerate(halves)
    ]
    for n in range(2):
        put(d_enc, activated.at[:, pl.ds(512 * n, 512)], 64 + 32 * n, stage_c, own_c)
    swap_c[1].start()
    for n in range(2):
        put(normed, d_pre.at[:, pl.ds(512 * n, 512)], 32 * n, stage_c, own_c)
    swap_c[0].start()
    for copy in (swap_c[1], swap_c[0]):
        copy.wait_recv()
    add(own_c, arrived_c)
    scatter_c = Scatter(own_c, 64, *ring_c)
    scatter_c.start()
    scatter_a.middle()
    scatter_b.middle()
    for half in range(2):
        first[pl.ds(128 * half, 128)] = scatter_a.finish(half)
    for half in range(2):
        second[pl.ds(32 * half, 32)] = scatter_b.finish(half)
    scatter_c.middle()
    scatter_a.drain()
    scatter_b.drain()
    across.drain()
    for copy in (swap_b, *swap_c):
        copy.wait_send()
    for half in range(2):
        second[pl.ds(64 + 64 * half, 64)] = scatter_c.finish(half)
    scatter_c.drain()


def run_weights(*args):
    sds = jax.ShapeDtypeStruct
    dma = pltpu.SemaphoreType.DMA
    return pl.pallas_call(
        weights_kernel,
        out_shape=(sds((256, 512), F32), sds((192, 512), F32)),
        in_specs=[VM] * 9,
        out_specs=(VM,) * 2,
        scratch_shapes=[
            *Scatter.scratch(128), *Scatter.scratch(32), *Scatter.scratch(64),
            pltpu.VMEM((256, 1024), BF), pltpu.VMEM((3, 64, 1024), BF), pltpu.VMEM((256, 1024), BF),
            dma((3,)), dma((3,)), dma((3,)), dma((3,)),
            pltpu.VMEM((256, 1024), BF),
            *[pltpu.VMEM((4, 4, 64, 512), BF)] * 3, *[pltpu.VMEM((4, 4, 128, 512), BF)] * 3,
            dma((3,)), dma((3,)),
        ],
        compiler_params=pltpu.CompilerParams(
            collective_id=2, has_side_effects=True, vmem_limit_bytes=VMEM_LIMIT
        ),
        cost_estimate=pl.CostEstimate(flops=3 * 10**9, bytes_accessed=16 * 2**20, transcendentals=2**18),
        name="weights_scatter",
    )(*args)


def unpack_kernel(first, second, out_in, out, g_query, g_key, g_value, g_attn, g_in, g_out):
    out[...] = out_in[...]
    g_query[...] = first[pl.ds(0, 128)]
    g_attn[...] = first[pl.ds(128, 128)].T
    g_key[...] = second[pl.ds(0, 32)]
    g_value[...] = second[pl.ds(32, 32)]
    for n in range(2):
        cols = pl.ds(512 * n, 512)
        g_in[:, cols] = second[pl.ds(64 + 32 * n, 32)]
        g_out[cols, :] = second[pl.ds(128 + 32 * n, 32)].T


def run_unpack(first, second, out):
    sds = jax.ShapeDtypeStruct
    return pl.pallas_call(
        unpack_kernel,
        out_shape=(
            sds((256, 1024), BF), sds((128, 512), F32), sds((32, 512), F32), sds((32, 512), F32),
            sds((512, 128), F32), sds((32, 1024), F32), sds((1024, 32), F32),
        ),
        in_specs=[VM] * 3,
        out_specs=(VM,) * 7,
        name="unpack",
    )(first, second, out)


def shards(
    enc_in, enc_gain, w_in, w_out, w_key, w_value, dec_in, w_query, w_attn_out, cotangent, group_doc, doc_lengths,
):
    normed, pre_act, activated, enc_out, kv, q_all, dm_all = run_encoder(
        enc_in[0], enc_gain[None, :], w_in, w_out, w_key, w_value, dec_in[0], w_query, w_attn_out, cotangent[0]
    )
    md, d_kv = run_attention(group_doc, doc_lengths, q_all, dm_all, kv)
    out, grads, kv_grad = run_decoder(d_kv, md, dec_in[0], cotangent[0], w_attn_out)
    first, second = run_weights(
        grads.reshape(4, 4, 256, 512), kv_grad, enc_out, normed, pre_act, activated, w_key, w_value, w_out
    )
    out, g_query, g_key, g_value, g_attn, g_in, g_out = run_unpack(first, second, out)
    return (out[None], g_query, g_key, g_value, g_attn, g_in, g_out)


def solution(mesh):
    placed = (
        P("grp", "seq", None),
        P(),
        P(None, "head"),
        P("head", None),
        P(None, "head"),
        P(None, "head"),
        P("grp", "seq", None),
        P(None, "head"),
        P("head", None),
        P("grp", "seq", None),
        P("grp", None),
        P("grp", None),
    )
    return jax.shard_map(
        shards,
        mesh=mesh,
        in_specs=placed,
        out_specs=(
            P("grp", "seq", "head"),
            P(("grp", "seq"), "head"),
            P(("grp", "seq"), "head"),
            P(("grp", "seq"), "head"),
            P("head", ("grp", "seq")),
            P(("grp", "seq"), "head"),
            P("head", ("grp", "seq")),
        ),
        check_vma=False,
    )
```

time: 359 us -> 186 us (0.52)
  Pallas kernels: 346 us -> 183 us
  other arithmetic: 6.01 us -> 0 us
  local copies, waits for them, and re-layouts: 6.47 us -> 1.87 us
    pallas_call x1, Pallas kernels: 108 us -> 40.7 us  [run_decoder(): pl.pallas_call(decoder_kernel, out_shape=(sds((256, 1024), BF), sds((16,...]
    pallas_call x1, Pallas kernels: 122 us -> 65.4 us  [run_weights(): pl.pallas_call(weights_kernel, out_shape=(sds((256, 512), F32), sds((192,...]
    pallas_call x1, Pallas kernels: 102 us -> 54.2 us  [run_encoder(): pl.pallas_call(encoder_kernel, out_shape=(sds((256, 1024), BF), sds((256,...]
    pallas_call x1 -> x2, Pallas kernels: 14.2 us -> 22.8 us  [the longest x1 20.1 us: run_attention(): pl.pallas_call(attention_kernel, out_shape=(sds((4, 256, 256), BF), sds((...]
where the time goes in v2:
time: 186 us
  Pallas kernels  183 us (98%)
  local copies, waits for them, and re-layouts  1.87 us (1%)
    pallas_call x1, Pallas kernels, run_weights(): pl.pallas_call(weights_kernel, out_shape=(sds((256, 512), F32), sds((192,...  65.4 us
    pallas_call x1, Pallas kernels, run_encoder(): pl.pallas_call(encoder_kernel, out_shape=(sds((256, 1024), BF), sds((256,...  54.2 us
    pallas_call x1, Pallas kernels, run_decoder(): pl.pallas_call(decoder_kernel, out_shape=(sds((256, 1024), BF), sds((16,...  40.7 us
    pallas_call x1, Pallas kernels, run_attention(): pl.pallas_call(attention_kernel, out_shape=(sds((4, 256, 256), BF), sds((...  20.1 us

profile of v2, /device:TPU:0, one launch (start us, length us, event | category | flops | bytes accessed | tf_op | source)
XLA Modules:
  0.0 185.7 jit_solution(15265669042064751442)
XLA Ops:
  0.6 54.2 %encoder_gather.1 = (bf16[256,1024]{1,0:T(8,128)(2,1)}, f32[256,1024]{1,0:T(8,128)}, bf16[256,1024]{1,0:T(8,128)(2,1)}, bf16[256,1024]{1,0:T(8,128)(2,1)}, bf16[...) custom-call(bf16[256,1024]{1,0:T(8,128)(2,1)} %bitcast.11, ...), custom_call_target="tpu_custom_call" | custom-call | flops 5000000000 | bytes 25165824 | tf_op jit(solution)/shard_map/encoder_gather/pallas_call | solution.py:351
  54.8 20.1 %attention.1 = (bf16[4,256,256]{2,1,0:T(8,128)(2,1)}, bf16[16,256,256]{2,1,0:T(8,128)(2,1)}) custom-call(s32[1,16]{1,0:T(1,128)} %group_doc.1, s32[1,8]{1,0:T(1,128)} %doc_lengths.1, bf16[4,256,128]{2,1,0:T(8,128)(2,1)} %get-tuple-element.28.q_all, bf16[4,256,128]{2,1,0:T(8,128)(2,1)} %get-tuple-element.29.dm_all, bf16[16,256,256]{2,1,0:T(8,128)(2,1)} %get-tuple-element.30.kv), custom_call_target="tpu_custom_call" | custom-call | flops 2000000000 | bytes 6291456 | tf_op jit(solution)/shard_map/attention/pallas_call | solution.py:460
  74.9 40.7 %decoder_scatter.1 = (bf16[256,1024]{1,0:T(8,128)(2,1)}, bf16[16,256,512]{2,1,0:T(8,128)(2,1)}, bf16[256,1024]{1,0:T(8,128)(2,1)}) custom-call(bf16[16,256,256]{2,1,0:T(8,128)(2,1)} %get-tuple-element.31.d_kv, bf16[4,256,256]{2,1,0:T(8,128)(2,1)} %get-tuple-element.32.md, bf16[256,4096]{1,0:T(8,128)(2,1)} %bitcast.8, bf16[256,4096]{1,0:T(8,128)(2,1)} %bitcast.10, ...), custom_call_target="tpu_custom_call" | custom-call | flops 4000000000 | bytes 20971520 | tf_op jit(solution)/shard_map/decoder_scatter/pallas_call | solution.py:596
  115.6 65.4 %weights_scatter.1 = (f32[256,512]{1,0:T(8,128)}, f32[192,512]{1,0:T(8,128)}) custom-call(bf16[4,4,256,512]{3,2,1,0:T(8,128)(2,1)} %bitcast.6, bf16[256,1024]{1,0:T(8,128)(2,1)} %get-tuple-element.34.kv_grad, bf16[256,1024]{1,0:T(8,128)(2,1)} %get-tuple-element.35.enc_out, bf16[256,1024]{1,0:T(8,128)(2,1)} %get-tuple-element.36.normed, ...), custom_call_target="tpu_custom_call" | custom-call | flops 3000000000 | bytes 16777216 | tf_op jit(solution)/shard_map/weights_scatter/pallas_call | solution.py:711
  181.0 2.8 %unpack.1 = (bf16[256,1024]{1,0:T(8,128)(2,1)}, f32[128,512]{1,0:T(8,128)}, f32[32,512]{1,0:T(8,128)}, f32[32,512]{1,0:T(8,128)}, f32[512,128]{1,0:T(8,128)}, /*index=5*/f32[32,1024]{1,0:T(8,128)}, f32[1024,32]{1,0:T(8,128)}) custom-call(f32[256,512]{1,0:T(8,128)} %get-tuple-element.39.first, f32[192,512]{1,0:T(8,128)} %get-tuple-element.40.second, ...), custom_call_target="tpu_custom_call" | custom-call | tf_op jit(solution)/shard_map/unpack/pallas_call | solution.py:746
  183.8 1.9 %copy.19 = f32[1024,32]{0,1:T(8,128)} copy(f32[1024,32]{1,0:T(8,128)} %get-tuple-element.55) | data formatting | bytes 262144

commit v3 on v2

--- a/solution.py
+++ b/solution.py
@@ -40,28 +40,46 @@
     return s >> 2, s & 3
 
 
-def x_copy(d, src, dst, send_sem, recv_sem):
+def device_at(along, across):
+    grp = lax.axis_index("grp")
+    return (4 - 3 * grp) * along + (1 + 3 * grp) * across
+
+
+def role():
     z, x = place()
+    grp = lax.axis_index("grp")
+    return (1 - grp) * z + grp * x, (1 - grp) * x + grp * z
+
+
+def seq_copy(peer, src, dst, send_sem, recv_sem):
     return pltpu.make_async_remote_copy(
         src_ref=src,
         dst_ref=dst,
         send_sem=send_sem,
         recv_sem=recv_sem,
-        device_id={"seq": 4 * z + ((x + d) & 3)},
+        device_id={"seq": peer},
         device_id_type=MESH,
     )
 
 
-def z_copy(d, src, dst, send_sem, recv_sem):
+def x_copy(d, *rest):
     z, x = place()
-    return pltpu.make_async_remote_copy(
-        src_ref=src,
-        dst_ref=dst,
-        send_sem=send_sem,
-        recv_sem=recv_sem,
-        device_id={"seq": 4 * ((z + d) & 3) + x},
-        device_id_type=MESH,
-    )
+    return seq_copy(4 * z + ((x + d) & 3), *rest)
+
+
+def z_copy(d, *rest):
+    z, x = place()
+    return seq_copy(4 * ((z + d) & 3) + x, *rest)
+
+
+def across_copy(d, *rest):
+    along, across = role()
+    return seq_copy(device_at(along, (across + d) & 3), *rest)
+
+
+def along_copy(d, *rest):
+    along, across = role()
+    return seq_copy(device_at((along + d) & 3, across), *rest)
 
 
 def greet(with_partner):
@@ -99,15 +117,15 @@
 class Swap:
     def __init__(self, source, target, ss, rs):
         self.source, self.target, self.ss, self.rs = source, target, ss, rs
-        self.x = place()[1]
+        self.x = role()[1]
 
     def sending(self, d):
         src = self.source.at[(self.x + d) & 3]
-        return x_copy(d, src, self.target.at[self.x], self.ss.at[d - 1], self.rs.at[d - 1])
+        return across_copy(d, src, self.target.at[self.x], self.ss.at[d - 1], self.rs.at[d - 1])
 
     def landing(self, d):
         ref = self.target.at[(self.x + 4 - d) & 3]
-        return x_copy(d, ref, ref, self.ss.at[d - 1], self.rs.at[d - 1])
+        return across_copy(d, ref, ref, self.ss.at[d - 1], self.rs.at[d - 1])
 
     def start(self):
         for d in (2, 1, 3):
@@ -132,16 +150,18 @@
         self.ss, self.rs, self.ss2, self.rs2 = ss, rs, ss2, rs2
         self.z, self.x = place()
 
-    def cut(self, half, d):
+    def cut(self, half, d, chunk):
         rows = pl.ds(half * self.n, self.n)
+        two = pl.ds(2 * chunk, 2)
         if half == 0:
-            return self.blocks.at[:, (self.x + d) & 3, rows]
-        return self.blocks.at[(self.z + d) & 3, :, rows]
-
-    def first(self, half, d):
+            return self.blocks.at[two, (self.x + d) & 3, rows]
+        return self.blocks.at[(self.z + d) & 3, two, rows]
+
+    def first(self, half, d, chunk):
         move = x_copy if half == 0 else z_copy
         return move(
-            d, self.cut(half, d), self.slots.at[half, d - 1], self.ss.at[half, d - 1], self.rs.at[half, d - 1]
+            d, self.cut(half, d, chunk), self.slots.at[half, d - 1, pl.ds(2 * chunk, 2)],
+            self.ss.at[half, d - 1, chunk], self.rs.at[half, d - 1, chunk],
         )
 
     def second(self, half, d):
@@ -152,24 +172,26 @@
             self.ss2.at[half, d - 1], self.rs2.at[half, d - 1],
         )
 
-    def start(self):
+    def start(self, half, chunk):
         for d in (2, 1, 3):
+            self.first(half, d, chunk).start()
+
+    def start_all(self):
+        for chunk in (0, 1):
             for half in (0, 1):
-                self.first(half, d).start()
-
-    def middle(self):
-        for half in (0, 1):
-            for d in (1, 3, 2):
-                self.first(half, d).wait_recv()
-            own = self.cut(half, 0)
-
-            def add(k, c):
-                total = own[k].astype(F32) + self.slots[half, 0, k].astype(F32)
-                total = total + self.slots[half, 1, k].astype(F32) + self.slots[half, 2, k].astype(F32)
-                self.sums[half, k] = total.astype(BF)
-                return c
-
-            lax.fori_loop(0, 4, add, 0)
+                self.start(half, chunk)
+
+    def middle(self, halves=(0, 1)):
+        for half in halves:
+            for chunk in (0, 1):
+                for d in (1, 3, 2):
+                    self.first(half, d, chunk).wait_recv()
+                own = self.cut(half, 0, chunk)
+                for k in range(2):
+                    total = own[k].astype(F32)
+                    for d in range(3):
+                        total = total + self.slots[half, d, 2 * chunk + k].astype(F32)
+                    self.sums[half, 2 * chunk + k] = total.astype(BF)
             for d in (2, 1, 3):
                 self.second(half, d).start()
 
@@ -185,7 +207,8 @@
     def drain(self):
         for half in (0, 1):
             for d in (1, 2, 3):
-                self.first(half, d).wait_send()
+                for chunk in (0, 1):
+                    self.first(half, d, chunk).wait_send()
                 self.second(half, d).wait_send()
 
     @staticmethod
@@ -193,7 +216,7 @@
         dma = pltpu.SemaphoreType.DMA
         return [
             pltpu.VMEM((2, 3, 4, n, 512), BF), pltpu.VMEM((2, 4, n, 512), BF), pltpu.VMEM((2, 3, n, 512), BF),
-            dma((2, 3)), dma((2, 3)), dma((2, 3)), dma((2, 3)),
+            dma((2, 3, 2)), dma((2, 3, 2)), dma((2, 3)), dma((2, 3)),
         ]
 
 
@@ -271,7 +294,7 @@
     greet(False)
     for copy in loads.values():
         copy.start()
-    z, x = place()
+    along, across_at = role()
     encoded = enc_in[...].astype(F32)
     square = jnp.mean(encoded * encoded, axis=1, keepdims=True)
     normed[...] = (encoded * lax.rsqrt(square + EPSILON) * gain[...]).astype(BF)
@@ -290,7 +313,7 @@
     across.send()
     q_swap = Swap(q_send, q_all, qs, qr)
     dm_swap = Swap(dm_send, dm_all, ds, dr)
-    kv_swap = Swap(kv_send, kv.at[pl.ds(4 * z, 4)], ks, kr)
+    kv_swap = Swap(kv_send, kv.at[pl.ds(4 * along, 4)], ks, kr)
     loads[id(v_dec)].wait()
     loads[id(v_query)].wait()
     for n in range(2):
@@ -316,12 +339,12 @@
     kv_swap.keep()
 
     def forward(k, d):
-        ref = kv.at[4 * z + ((x + k) & 3)]
-        return z_copy(d, ref, ref, zs.at[d - 1, k], zr.at[d - 1, k])
+        ref = kv.at[4 * along + ((across_at + k) & 3)]
+        return along_copy(d, ref, ref, zs.at[d - 1, k], zr.at[d - 1, k])
 
     def arriving(k, d):
-        ref = kv.at[4 * ((z + 4 - d) & 3) + ((x + k) & 3)]
-        return z_copy(d, ref, ref, zs.at[d - 1, k], zr.at[d - 1, k])
+        ref = kv.at[4 * ((along + 4 - d) & 3) + ((across_at + k) & 3)]
+        return along_copy(d, ref, ref, zs.at[d - 1, k], zr.at[d - 1, k])
 
     for d in (2, 1, 3):
         forward(0, d).start()
@@ -375,7 +398,7 @@
 
 
 def attention_kernel(group_doc, doc_lengths, q_all, dm_all, kv, md, d_kv, scores, acc, d_acc, ends, begins, limits):
-    z = lax.axis_index("seq") >> 2
+    along = role()[0]
     total = 0
     for j in range(8):
         total = total + doc_lengths[0, j]
@@ -386,7 +409,7 @@
         begins[g] = ends[doc] - doc_lengths[0, doc]
     bounds = []
     for b in range(4):
-        origin = z * 1024 + b * 256
+        origin = device_at(along, b) * 256
         lo, hi = 0, 0
         for g in range(N_SEQ):
             lo = lo + jnp.where(limits[g] <= origin, 1, 0)
@@ -394,6 +417,9 @@
         bounds.append((origin, lo, hi))
     low, high = bounds[0][1], bounds[3][2]
 
+    def at(g):
+        return device_at(g >> 2, g & 3)
+
     def clear(g, c):
         inside = (g >= low) & (g < high)
 
@@ -403,7 +429,7 @@
 
         @pl.when(jnp.logical_not(inside))
         def _():
-            d_kv[g] = jnp.zeros((256, 256), BF)
+            d_kv[at(g)] = jnp.zeros((256, 256), BF)
 
         return c
 
@@ -413,7 +439,7 @@
         position = origin + lax.broadcasted_iota(jnp.int32, (256, 1), 0)
 
         def score(g, m):
-            s = mm_cols(q_all[b], kv[g, :, pl.ds(0, 128)]) * SCALE
+            s = mm_cols(q_all[b], kv[at(g), :, pl.ds(0, 128)]) * SCALE
             seen = (position >= begins[g]) & (position < limits[g])
             s = jnp.where(seen, s, MASKED)
             scores[g] = s
@@ -425,7 +451,7 @@
         def weigh(g, total):
             p = jnp.exp(scores[g] - top)
             scores[g] = p
-            acc[...] += mm(p.astype(BF), kv[g, :, pl.ds(128, 128)])
+            acc[...] += mm(p.astype(BF), kv[at(g), :, pl.ds(128, 128)])
             return total + jnp.sum(p, axis=1, keepdims=True)
 
         total = lax.fori_loop(lo, hi, weigh, jnp.zeros((256, 1), F32))
@@ -437,9 +463,9 @@
 
         def back(g, c):
             p = scores[g] * inverse
-            dw = mm_cols(dm_all[b], kv[g, :, pl.ds(128, 128)])
+            dw = mm_cols(dm_all[b], kv[at(g), :, pl.ds(128, 128)])
             ds = (p * (dw - inner) * SCALE).astype(BF)
-            acc[...] += mm(ds, kv[g, :, pl.ds(0, 128)])
+            acc[...] += mm(ds, kv[at(g), :, pl.ds(0, 128)])
             d_acc[g, :, pl.ds(0, 128)] += mm_rows(ds, q_all[b])
             d_acc[g, :, pl.ds(128, 128)] += mm_rows(p.astype(BF), dm_all[b])
             return c
@@ -448,7 +474,7 @@
         md[b, :, pl.ds(128, 128)] = acc[...].astype(BF)
 
     def settle(g, c):
-        d_kv[g] = d_acc[g].astype(BF)
+        d_kv[at(g)] = d_acc[g].astype(BF)
         return c
 
     lax.fori_loop(low, high, settle, 0)
@@ -473,29 +499,40 @@
 
 
 def decoder_kernel(
-    d_kv, md, dec, cot, w_attn,
-    out, grads, kv_grad,
-    v_dec, v_cot, v_attn, load_sem,
-    m_all, ms, mr, row_slots, zs, zr, row, kvg, ks, kr, mixed, d_query,
-    out_own, out_send, out_recv, os, orr, stage, arrived, ps, pr,
+    d_kv, md, dec, cot, w_attn, w_key, w_value, w_out, enc_out, normed, activated, pre_act,
+    out, first, second,
+    *scratch,
 ):
+    ring_a, ring_b, ring_c = scratch[0:7], scratch[7:14], scratch[14:21]
+    v_dec, v_cot, v_attn, v_key, v_value, v_out, v_enc, v_normed, v_act, v_pre, load_sem = scratch[21:32]
+    (
+        m_all, ms, mr, row_slots, zs, zr, row, kvg, ks, kr, mixed, d_query,
+        out_own, out_send, out_recv, os, orr, stage, arrived, ps, pr,
+    ) = scratch[32:53]
+    (
+        k_grad, v_grad, parts, slots, d_enc, hs1, hr1, hs2, hr2, d_pre,
+        own_b, stage_b, arrived_b, own_c, stage_c, arrived_c, cs, cr,
+    ) = scratch[53:]
     greet(True)
     loads = [
         pltpu.make_async_copy(a, v, load_sem.at[i])
-        for i, (a, v) in enumerate(((w_attn, v_attn), (dec, v_dec), (cot, v_cot)))
+        for i, (a, v) in enumerate((
+            (w_attn, v_attn), (dec, v_dec), (cot, v_cot), (w_key, v_key), (w_value, v_value),
+            (enc_out, v_enc), (w_out, v_out), (pre_act, v_pre), (activated, v_act), (normed, v_normed),
+        ))
     ]
     for load in loads:
         load.start()
     met(True)
-    z, x = place()
+    along, across_at = role()
     h = lax.axis_index("head")
     grp = lax.axis_index("grp")
     m_swap = Swap(md, m_all, ms, mr)
     kv_swap = Swap(row, kvg, ks, kr)
 
     def term(k, d):
-        src = d_kv.at[4 * ((z + d) & 3) + ((x + k) & 3)]
-        return z_copy(d, src, row_slots.at[d - 1, k], zs.at[d - 1, k], zr.at[d - 1, k])
+        src = d_kv.at[4 * ((along + d) & 3) + ((across_at + k) & 3)]
+        return along_copy(d, src, row_slots.at[d - 1, k], zs.at[d - 1, k], zr.at[d - 1, k])
 
     m_swap.start()
     for k in (2, 1, 3, 0):
@@ -510,14 +547,14 @@
     def out_copy(d):
         return head_copy(d, out_send.at[d - 1], out_recv.at[d - 1], os, orr)
 
-    def part(n, first):
-        return pl.ds(pl.multiple_of(first + n * 256, 256), 256)
+    def part(n, start):
+        return pl.ds(pl.multiple_of(start + n * 256, 256), 256)
 
     loads[0].wait()
     for d in (2, 1, 3):
-        first = ((h + d) & 3) * 1024
+        start = ((h + d) & 3) * 1024
         for n in range(4):
-            out_send[d - 1, :, pl.ds(n * 256, 256)] = mm(mixed[...], v_attn[:, part(n, first)]).astype(BF)
+            out_send[d - 1, :, pl.ds(n * 256, 256)] = mm(mixed[...], v_attn[:, part(n, start)]).astype(BF)
         out_copy(d).start()
     loads[1].wait()
     loads[2].wait()
@@ -528,37 +565,20 @@
         return mm_rows(v_dec[:, here], d_query[...]), mm_rows(v_cot[:, here], mixed[...])
 
     def exchange(u):
-        pair = pl.ds(2 * u, 2)
-        return partner_copy(stage.at[pair], arrived.at[pair], ps.at[u], pr.at[u])
+        place_u = (u >> 1, pl.ds(2 * (u & 1), 2))
+        return partner_copy(stage.at[place_u], arrived.at[place_u], ps.at[u], pr.at[u])
 
     def far(u, c):
         for which, value in enumerate(products(u)):
             for k in range(2):
-                stage[2 * u + k, pl.ds(128 * which, 128)] = value[128 * k : 128 * (k + 1)].astype(BF)
+                stage[u >> 1, 2 * (u & 1) + k, pl.ds(128 * which, 128)] = value[128 * k : 128 * (k + 1)].astype(BF)
         exchange(u).start()
         return c
 
     lax.fori_loop(0, 8, far, 0)
-
-    for n in range(4):
-        here = part(n, h * 1024)
-        out_own[:, pl.ds(n * 256, 256)] = mm(mixed[...], v_attn[:, here]) + v_dec[:, here].astype(F32)
-
-    def near(u, c):
-        values = products(u + 8)
-        exchange(u).wait_recv()
-        for which, value in enumerate(values):
-            for k in range(2):
-                rows = pl.ds(128 * which, 128)
-                both = value[128 * k : 128 * (k + 1)] + arrived[2 * u + k, rows].astype(F32)
-                grads[2 * u + k, rows] = both.astype(BF)
-        return c
-
-    lax.fori_loop(0, 8, near, 0)
-
     for k in (2, 1, 3, 0):
-        there = (x + k) & 3
-        total = d_kv[4 * z + there].astype(F32)
+        there = (across_at + k) & 3
+        total = d_kv[4 * along + there].astype(F32)
         for d in (1, 3, 2):
             term(k, d).wait_recv()
             total = total + row_slots[d - 1, k].astype(F32)
@@ -566,15 +586,102 @@
         if k:
             kv_swap.sending(k).start()
     kv_swap.keep()
+
+    def near(u, c):
+        values = products(u + 8)
+        exchange(u).wait_recv()
+        for which, value in enumerate(values):
+            for k in range(2):
+                rows = pl.ds(128 * which, 128)
+                block = 2 * (u & 1) + k
+                both = value[128 * k : 128 * (k + 1)] + arrived[u >> 1, block, rows].astype(F32)
+                arrived[u >> 1, block, rows] = both.astype(BF)
+        return c
+
+    lax.fori_loop(0, 8, near, 0)
+    scatter_a = Scatter(arrived, 128, *ring_a)
+    scatter_a.start_all()
+    kv_swap.finish()
+    for j in range(4):
+        k_grad[:, pl.ds(128 * j, 128)] = kvg[j, :, pl.ds(0, 128)]
+        v_grad[:, pl.ds(128 * j, 128)] = kvg[j, :, pl.ds(128, 128)]
+    loads[3].wait()
+    loads[4].wait()
+    for n in range(4):
+        rows = pl.ds(n * 256, 256)
+        value = mm_cols(k_grad[...], v_key[rows, :]) + mm_cols(v_grad[...], v_value[rows, :])
+        parts[:, rows] = value.astype(BF)
+    total_d = HeadSum(parts, slots, d_enc, hs1, hr1, hs2, hr2)
+    total_d.send()
+
+    for n in range(4):
+        here = part(n, h * 1024)
+        out_own[:, pl.ds(n * 256, 256)] = mm(mixed[...], v_attn[:, here]) + v_dec[:, here].astype(F32)
+    far_from, near_from = (1 - grp) * 512, grp * 512
+
+    def put(left, right, row_at, far_to, near_to):
+        for base, target in ((far_from, far_to), (near_from, near_to)):
+            for n in range(2):
+                cols = part(n, base)
+                value = mm_rows(left[:, cols], right[...])
+                for k in range(8):
+                    block = n * 8 + k
+                    target[block // 4, block % 4, pl.ds(row_at, 32)] = value[32 * k : 32 * (k + 1)].astype(BF)
+
+    def add(own, more):
+        def body(b, c):
+            own[b] = (own[b].astype(F32) + more[b].astype(F32)).astype(BF)
+            return c
+
+        lax.fori_loop(0, 4, body, 0)
+
+    loads[5].wait()
+    swap_b = partner_copy(stage_b, arrived_b, cs.at[0], cr.at[0])
+    put(v_enc, k_grad, 0, stage_b, own_b)
+    put(v_enc, v_grad, 32, stage_b, own_b)
+    swap_b.start()
+    total_d.share(total_d.receive())
+    swap_b.wait_recv()
+    add(own_b, arrived_b)
+    scatter_b = Scatter(own_b, 32, *ring_b)
+    scatter_b.start_all()
     total = out_own[...]
     for d in (1, 3, 2):
         out_copy(d).wait_recv()
         total = total + out_recv[d - 1].astype(F32)
     out[...] = total.astype(BF)
-    kv_swap.finish()
-    for j in range(4):
-        kv_grad[:, pl.ds(128 * j, 128)] = kvg[j, :, pl.ds(0, 128)]
-        kv_grad[:, pl.ds(512 + 128 * j, 128)] = kvg[j, :, pl.ds(128, 128)]
+    for load in loads[6:]:
+        load.wait()
+    total_d.collect()
+    for n in range(4):
+        cols = pl.ds(n * 256, 256)
+        pre = v_pre[:, cols]
+        sig = 1.0 / (1.0 + jnp.exp(-pre))
+        slope = sig * (1.0 + pre * (1.0 - sig))
+        d_pre[:, cols] = (mm_cols(d_enc[...], v_out[cols, :]) * slope).astype(BF)
+    halves = [pl.ds(64 * which, 64) for which in range(2)]
+    swap_c = [
+        partner_copy(stage_c.at[:, :, r], arrived_c.at[:, :, r], cs.at[1 + i], cr.at[1 + i])
+        for i, r in enumerate(halves)
+    ]
+    for n in range(2):
+        put(d_enc, v_act.at[:, pl.ds(512 * n, 512)], 64 + 32 * n, stage_c, own_c)
+    swap_c[1].start()
+    for n in range(2):
+        put(v_normed, d_pre.at[:, pl.ds(512 * n, 512)], 32 * n, stage_c, own_c)
+    swap_c[0].start()
+    scatter_a.middle()
+    for copy in (swap_c[1], swap_c[0]):
+        copy.wait_recv()
+    add(own_c, arrived_c)
+    scatter_c = Scatter(own_c, 64, *ring_c)
+    scatter_c.start_all()
+    scatter_b.middle()
+    for half in range(2):
+        first[pl.ds(128 * half, 128)] = scatter_a.finish(half)
+    for half in range(2):
+        second[pl.ds(32 * half, 32)] = scatter_b.finish(half)
+    scatter_c.middle()
     m_swap.drain()
     kv_swap.drain()
     for k in range(4):
@@ -588,6 +695,14 @@
         return c
 
     lax.fori_loop(0, 8, sent, 0)
+    scatter_a.drain()
+    scatter_b.drain()
+    total_d.drain()
+    for copy in (swap_b, *swap_c):
+        copy.wait_send()
+    for half in range(2):
+        second[pl.ds(64 + 64 * half, 64)] = scatter_c.finish(half)
+    scatter_c.drain()
 
 
 def run_decoder(*args):
@@ -595,126 +710,23 @@
     dma = pltpu.SemaphoreType.DMA
     return pl.pallas_call(
         decoder_kernel,
-        out_shape=(sds((256, 1024), BF), sds((16, 256, 512), BF), sds((256, 1024), BF)),
-        in_specs=[VM, VM, ANY, ANY, ANY],
+        out_shape=(sds((256, 1024), BF), sds((256, 512), F32), sds((192, 512), F32)),
+        in_specs=[VM, VM] + [ANY] * 10,
         out_specs=(VM,) * 3,
         scratch_shapes=[
-            pltpu.VMEM((256, 4096), BF), pltpu.VMEM((256, 4096), BF), pltpu.VMEM((512, 4096), BF), dma((3,)),
+            *Scatter.scratch(128), *Scatter.scratch(32), *Scatter.scratch(64),
+            pltpu.VMEM((256, 4096), BF), pltpu.VMEM((256, 4096), BF), pltpu.VMEM((512, 4096), BF),
+            pltpu.VMEM((1024, 512), BF), pltpu.VMEM((1024, 512), BF), pltpu.VMEM((1024, 1024), BF),
+            pltpu.VMEM((256, 1024), BF), pltpu.VMEM((256, 1024), BF), pltpu.VMEM((256, 1024), BF),
+            pltpu.VMEM((256, 1024), F32), dma((10,)),
             pltpu.VMEM((4, 256, 256), BF), dma((3,)), dma((3,)),
             pltpu.VMEM((3, 4, 256, 256), BF), dma((3, 4)), dma((3, 4)),
             pltpu.VMEM((4, 256, 256), BF), pltpu.VMEM((4, 256, 256), BF), dma((3,)), dma((3,)),
             pltpu.VMEM((256, 512), BF), pltpu.VMEM((256, 512), BF),
             pltpu.VMEM((256, 1024), F32), pltpu.VMEM((3, 256, 1024), BF), pltpu.VMEM((3, 256, 1024), BF),
             dma((3,)), dma((3,)),
-            pltpu.VMEM((16, 256, 512), BF), pltpu.VMEM((16, 256, 512), BF), dma((8,)), dma((8,)),
-        ],
-        compiler_params=pltpu.CompilerParams(
-            collective_id=1, has_side_effects=True, vmem_limit_bytes=VMEM_LIMIT
-        ),
-        cost_estimate=pl.CostEstimate(flops=4 * 10**9, bytes_accessed=20 * 2**20, transcendentals=0),
-        name="decoder_scatter",
-    )(*args)
-
-
-def weights_kernel(
-    grads, kv_grad, enc_out, normed, pre_act, activated, w_key, w_value, w_out,
-    first, second,
-    *scratch,
-):
-    ring_a, ring_b, ring_c = scratch[0:7], scratch[7:14], scratch[14:21]
-    (
-        parts, slots, d_enc, hs1, hr1, hs2, hr2, d_pre,
-        own_b, stage_b, arrived_b, own_c, stage_c, arrived_c, ps, pr,
-    ) = scratch[21:]
-    greet(True)
-    grp = lax.axis_index("grp")
-    k_grad, v_grad = kv_grad.at[:, pl.ds(0, 512)], kv_grad.at[:, pl.ds(512, 512)]
-    for n in range(4):
-        rows = pl.ds(n * 256, 256)
-        part = mm_cols(k_grad[...], w_key[rows, :]) + mm_cols(v_grad[...], w_value[rows, :])
-        parts[:, rows] = part.astype(BF)
-    met(True)
-    across = HeadSum(parts, slots, d_enc, hs1, hr1, hs2, hr2)
-    across.send()
-    scatter_a = Scatter(grads, 128, *ring_a)
-    scatter_a.start()
-    far, near = (1 - grp) * 512, grp * 512
-
-    def put(left, right, row, stage, own):
-        for base, target in ((far, stage), (near, own)):
-            for n in range(2):
-                cols = pl.ds(pl.multiple_of(base + n * 256, 256), 256)
-                value = mm_rows(left[:, cols], right[...])
-                for k in range(8):
-                    block = n * 8 + k
-                    target[block // 4, block % 4, pl.ds(row, 32)] = value[32 * k : 32 * (k + 1)].astype(BF)
-
-    def add(own, arrived):
-        def body(b, c):
-            own[b] = (own[b].astype(F32) + arrived[b].astype(F32)).astype(BF)
-            return c
-
-        lax.fori_loop(0, 4, body, 0)
-
-    swap_b = partner_copy(stage_b, arrived_b, ps.at[0], pr.at[0])
-    put(enc_out, k_grad, 0, stage_b, own_b)
-    put(enc_out, v_grad, 32, stage_b, own_b)
-    swap_b.start()
-    across.share(across.receive())
-    swap_b.wait_recv()
-    add(own_b, arrived_b)
-    scatter_b = Scatter(own_b, 32, *ring_b)
-    scatter_b.start()
-    across.collect()
-    for n in range(4):
-        cols = pl.ds(n * 256, 256)
-        pre = pre_act[:, cols]
-        sig = 1.0 / (1.0 + jnp.exp(-pre))
-        slope = sig * (1.0 + pre * (1.0 - sig))
-        d_pre[:, cols] = (mm_cols(d_enc[...], w_out[cols, :]) * slope).astype(BF)
-    halves = [pl.ds(64 * which, 64) for which in range(2)]
-    swap_c = [
-        partner_copy(stage_c.at[:, :, r], arrived_c.at[:, :, r], ps.at[1 + i], pr.at[1 + i])
-        for i, r in enumerate(halves)
-    ]
-    for n in range(2):
-        put(d_enc, activated.at[:, pl.ds(512 * n, 512)], 64 + 32 * n, stage_c, own_c)
-    swap_c[1].start()
-    for n in range(2):
-        put(normed, d_pre.at[:, pl.ds(512 * n, 512)], 32 * n, stage_c, own_c)
-    swap_c[0].start()
-    for copy in (swap_c[1], swap_c[0]):
-        copy.wait_recv()
-    add(own_c, arrived_c)
-    scatter_c = Scatter(own_c, 64, *ring_c)
-    scatter_c.start()
-    scatter_a.middle()
-    scatter_b.middle()
-    for half in range(2):
-        first[pl.ds(128 * half, 128)] = scatter_a.finish(half)
-    for half in range(2):
-        second[pl.ds(32 * half, 32)] = scatter_b.finish(half)
-    scatter_c.middle()
-    scatter_a.drain()
-    scatter_b.drain()
-    across.drain()
-    for copy in (swap_b, *swap_c):
-        copy.wait_send()
-    for half in range(2):
-        second[pl.ds(64 + 64 * half, 64)] = scatter_c.finish(half)
-    scatter_c.drain()
-
-
-def run_weights(*args):
-    sds = jax.ShapeDtypeStruct
-    dma = pltpu.SemaphoreType.DMA
-    return pl.pallas_call(
-        weights_kernel,
-        out_shape=(sds((256, 512), F32), sds((192, 512), F32)),
-        in_specs=[VM] * 9,
-        out_specs=(VM,) * 2,
-        scratch_shapes=[
-            *Scatter.scratch(128), *Scatter.scratch(32), *Scatter.scratch(64),
+            pltpu.VMEM((4, 4, 256, 512), BF), pltpu.VMEM((4, 4, 256, 512), BF), dma((8,)), dma((8,)),
+            pltpu.VMEM((256, 512), BF), pltpu.VMEM((256, 512), BF),
             pltpu.VMEM((256, 1024), BF), pltpu.VMEM((3, 64, 1024), BF), pltpu.VMEM((256, 1024), BF),
             dma((3,)), dma((3,)), dma((3,)), dma((3,)),
             pltpu.VMEM((256, 1024), BF),
@@ -722,10 +734,10 @@
             dma((3,)), dma((3,)),
         ],
         compiler_params=pltpu.CompilerParams(
-            collective_id=2, has_side_effects=True, vmem_limit_bytes=VMEM_LIMIT
+            collective_id=1, has_side_effects=True, vmem_limit_bytes=VMEM_LIMIT
         ),
-        cost_estimate=pl.CostEstimate(flops=3 * 10**9, bytes_accessed=16 * 2**20, transcendentals=2**18),
-        name="weights_scatter",
+        cost_estimate=pl.CostEstimate(flops=7 * 10**9, bytes_accessed=24 * 2**20, transcendentals=2**18),
+        name="decoder_scatter",
     )(*args)
 
 
@@ -738,7 +750,7 @@
     for n in range(2):
         cols = pl.ds(512 * n, 512)
         g_in[:, cols] = second[pl.ds(64 + 32 * n, 32)]
-        g_out[cols, :] = second[pl.ds(128 + 32 * n, 32)].T
+        g_out[:, cols] = second[pl.ds(128 + 32 * n, 32)]
 
 
 def run_unpack(first, second, out):
@@ -747,7 +759,7 @@
         unpack_kernel,
         out_shape=(
             sds((256, 1024), BF), sds((128, 512), F32), sds((32, 512), F32), sds((32, 512), F32),
-            sds((512, 128), F32), sds((32, 1024), F32), sds((1024, 32), F32),
+            sds((512, 128), F32), sds((32, 1024), F32), sds((32, 1024), F32),
         ),
         in_specs=[VM] * 3,
         out_specs=(VM,) * 7,
@@ -762,12 +774,11 @@
         enc_in[0], enc_gain[None, :], w_in, w_out, w_key, w_value, dec_in[0], w_query, w_attn_out, cotangent[0]
     )
     md, d_kv = run_attention(group_doc, doc_lengths, q_all, dm_all, kv)
-    out, grads, kv_grad = run_decoder(d_kv, md, dec_in[0], cotangent[0], w_attn_out)
-    first, second = run_weights(
-        grads.reshape(4, 4, 256, 512), kv_grad, enc_out, normed, pre_act, activated, w_key, w_value, w_out
+    out, first, second = run_decoder(
+        d_kv, md, dec_in[0], cotangent[0], w_attn_out, w_key, w_value, w_out, enc_out, normed, activated, pre_act
     )
     out, g_query, g_key, g_value, g_attn, g_in, g_out = run_unpack(first, second, out)
-    return (out[None], g_query, g_key, g_value, g_attn, g_in, g_out)
+    return (out[None], g_query, g_key, g_value, g_attn, g_in, g_out.T)
 
 
 def solution(mesh):

time: 186 us -> 153 us (0.82)
  Pallas kernels: 183 us -> 153 us
  local copies, waits for them, and re-layouts: 1.87 us -> 0 us
    pallas_call x2 -> x1, Pallas kernels: 106 us -> 78.7 us  [run_decoder(): pl.pallas_call(decoder_kernel, out_shape=(sds((256, 1024), BF), sds((256,...]
    pallas_call x1, Pallas kernels: 54.2 us -> 46.4 us  [run_encoder(): pl.pallas_call(encoder_kernel, out_shape=(sds((256, 1024), BF), sds((256,...]
    pallas_call x1, Pallas kernels: 20.1 us -> 25 us  [run_attention(): pl.pallas_call(attention_kernel, out_shape=(sds((4, 256, 256), BF), sds((...]
    unnamed x1 -> x0, local copies, waits for them, and re-layouts: 1.87 us -> none
where the time goes in v3:
time: 153 us
  Pallas kernels  153 us (100%)
    pallas_call x1, Pallas kernels, run_decoder(): pl.pallas_call(decoder_kernel, out_shape=(sds((256, 1024), BF), sds((256,...  78.7 us
    pallas_call x1, Pallas kernels, run_encoder(): pl.pallas_call(encoder_kernel, out_shape=(sds((256, 1024), BF), sds((256,...  46.4 us
    pallas_call x1, Pallas kernels, run_attention(): pl.pallas_call(attention_kernel, out_shape=(sds((4, 256, 256), BF), sds((...  25 us

profile of v3, /device:TPU:0, one launch (start us, length us, event | category | flops | bytes accessed | tf_op | source)
XLA Modules:
  0.0 153.2 jit_solution(9104687495341607943)
XLA Ops:
  0.6 46.4 %encoder_gather.1 = (bf16[256,1024]{1,0:T(8,128)(2,1)}, f32[256,1024]{1,0:T(8,128)}, bf16[256,1024]{1,0:T(8,128)(2,1)}, bf16[256,1024]{1,0:T(8,128)(2,1)}, bf16[...) custom-call(bf16[256,1024]{1,0:T(8,128)(2,1)} %bitcast.10, ...), custom_call_target="tpu_custom_call" | custom-call | flops 5000000000 | bytes 25165824 | tf_op jit(solution)/shard_map/encoder_gather/pallas_call | solution.py:374
  47.0 25.0 %attention.1 = (bf16[4,256,256]{2,1,0:T(8,128)(2,1)}, bf16[16,256,256]{2,1,0:T(8,128)(2,1)}) custom-call(s32[1,16]{1,0:T(1,128)} %group_doc.1, s32[1,8]{1,0:T(1,128)} %doc_lengths.1, bf16[4,256,128]{2,1,0:T(8,128)(2,1)} %get-tuple-element.26.q_all, bf16[4,256,128]{2,1,0:T(8,128)(2,1)} %get-tuple-element.27.dm_all, bf16[16,256,256]{2,1,0:T(8,128)(2,1)} %get-tuple-element.28.kv), custom_call_target="tpu_custom_call" | custom-call | flops 2000000000 | bytes 6291456 | tf_op jit(solution)/shard_map/attention/pallas_call | solution.py:486
  72.0 78.7 %decoder_scatter.1 = (bf16[256,1024]{1,0:T(8,128)(2,1)}, f32[256,512]{1,0:T(8,128)}, f32[192,512]{1,0:T(8,128)}) custom-call(bf16[16,256,256]{2,1,0:T(8,128)(2,1)} %get-tuple-element.29.d_kv, bf16[4,256,256]{2,1,0:T(8,128)(2,1)} %get-tuple-element.30.md, bf16[256,4096]{1,0:T(8,128)(2,1)} %bitcast.7, bf16[256,4096]{1,0:T(8,128)(2,1)} %bitcast.9, ...), custom_call_target="tpu_custom_call" | custom-call | flops 7000000000 | bytes 25165824 | tf_op jit(solution)/shard_map/decoder_scatter/pallas_call | solution.py:711
  150.8 2.5 %unpack.1 = (bf16[256,1024]{1,0:T(8,128)(2,1)}, f32[128,512]{1,0:T(8,128)}, f32[32,512]{1,0:T(8,128)}, f32[32,512]{1,0:T(8,128)}, f32[512,128]{1,0:T(8,128)}, /*index=5*/f32[32,1024]{1,0:T(8,128)}, f32[32,1024]{1,0:T(8,128)}) custom-call(f32[256,512]{1,0:T(8,128)} %get-tuple-element.35.first, f32[192,512]{1,0:T(8,128)} %get-tuple-element.36.second, ...), custom_call_target="tpu_custom_call" | custom-call | tf_op jit(solution)/shard_map/unpack/pallas_call | solution.py:758

commit v4 on v3

--- a/solution.py
+++ b/solution.py
@@ -15,6 +15,7 @@
 EPSILON = 1e-06
 MASKED = -1e30
 SCALE = 1.0 / math.sqrt(HEAD_DIM)
+SCALE2 = SCALE * math.log2(math.e)
 MESH = pl.DeviceIdType.MESH
 BF = jnp.bfloat16
 F32 = jnp.float32
@@ -212,10 +213,10 @@
                 self.second(half, d).wait_send()
 
     @staticmethod
-    def scratch(n):
+    def scratch(n, c):
         dma = pltpu.SemaphoreType.DMA
         return [
-            pltpu.VMEM((2, 3, 4, n, 512), BF), pltpu.VMEM((2, 4, n, 512), BF), pltpu.VMEM((2, 3, n, 512), BF),
+            pltpu.VMEM((2, 3, 4, n, c), BF), pltpu.VMEM((2, 4, n, c), BF), pltpu.VMEM((2, 3, n, c), BF),
             dma((2, 3, 2)), dma((2, 3, 2)), dma((2, 3)), dma((2, 3)),
         ]
 
@@ -281,7 +282,8 @@
 
 def encoder_kernel(
     enc_in, gain, w_in, w_out, w_key, w_value, dec, w_query, w_attn, cot,
-    normed, pre_act, activated, enc_out, kv, q_all, dm_all,
+    normed_out, pre_out, act_out, enc_out_out, kv_out, q_out, dm_out,
+    normed, pre_act, activated, enc_out, kv, q_all, dm_all, store_sem, kv_sem,
     v_in, v_out, v_key, v_value, v_dec, v_query, v_attn, v_cot, load_sem,
     parts, slots, hs1, hr1, hs2, hr2,
     q_send, dm_send, kv_send, qs, qr, ds, dr, ks, kr, zs, zr,
@@ -291,6 +293,13 @@
         (w_key, v_key), (w_value, v_value), (cot, v_cot), (w_attn, v_attn),
     )
     loads = {id(v): pltpu.make_async_copy(a, v, load_sem.at[i]) for i, (a, v) in enumerate(pairs)}
+    stores = [
+        pltpu.make_async_copy(v, a, store_sem.at[i])
+        for i, (v, a) in enumerate((
+            (normed, normed_out), (pre_act, pre_out), (activated, act_out), (enc_out, enc_out_out),
+            (q_all, q_out), (dm_all, dm_out),
+        ))
+    ]
     greet(False)
     for copy in loads.values():
         copy.start()
@@ -309,6 +318,8 @@
         cols = pl.ds(n * 256, 256)
         parts[:, cols] = mm(activated[...], v_out[:, cols]).astype(BF)
     met(False)
+    for store in stores[:3]:
+        store.start()
     across = HeadSum(parts, slots, enc_out, hs1, hr1, hs2, hr2)
     across.send()
     q_swap = Swap(q_send, q_all, qs, qr)
@@ -338,34 +349,59 @@
     kv_swap.start()
     kv_swap.keep()
 
-    def forward(k, d):
-        ref = kv.at[4 * along + ((across_at + k) & 3)]
-        return along_copy(d, ref, ref, zs.at[d - 1, k], zr.at[d - 1, k])
-
-    def arriving(k, d):
-        ref = kv.at[4 * ((along + 4 - d) & 3) + ((across_at + k) & 3)]
-        return along_copy(d, ref, ref, zs.at[d - 1, k], zr.at[d - 1, k])
-
-    for d in (2, 1, 3):
-        forward(0, d).start()
+    def kv_part(k, back):
+        return kv.at[4 * ((along + 4 - back) & 3) + ((across_at + k) & 3)]
+
+    def move(k, d, back, slot):
+        ref = kv_part(k, back)
+        return along_copy(d, ref, ref, zs.at[slot, k], zr.at[slot, k])
+
+    def keep(k, back):
+        at = 4 * ((along + 4 - back) & 3) + ((across_at + k) & 3)
+        return pltpu.make_async_copy(kv.at[at], kv_out.at[at], kv_sem.at[back, k])
+
+    def ahead(k):
+        return 1 if k % 2 == 0 else 3
+
+    order = (0, 3, 1, 2)
+    for d in (1, 3):
+        move(0, d, 0, d - 1).start()
+    for k in order[1:]:
+        kv_swap.landing(4 - k).wait_recv()
+        for d in (ahead(k), 4 - ahead(k)):
+            move(k, d, 0, d - 1).start()
     dm_swap.start()
-    for k in (3, 1, 2):
-        kv_swap.landing(4 - k).wait_recv()
-        for d in (2, 1, 3):
-            forward(k, d).start()
-    q_swap.keep()
-    dm_swap.keep()
-    q_swap.finish()
-    dm_swap.finish()
-    for k in (0, 3, 1, 2):
-        for d in (1, 3, 2):
-            arriving(k, d).wait_recv()
-    for k in range(4):
-        for d in (1, 2, 3):
-            forward(k, d).wait_send()
+    for k in order:
+        keep(k, 0).start()
+        d = ahead(k)
+        move(k, d, d, d - 1).wait_recv()
+        move(k, d, d, 1).start()
+        keep(k, d).start()
+    across_at_rest = (q_swap, dm_swap)
+    stores[3].start()
+    for swap, store in zip(across_at_rest, stores[4:]):
+        swap.keep()
+        swap.finish()
+        store.start()
+    for k in order:
+        d = 4 - ahead(k)
+        move(k, d, d, d - 1).wait_recv()
+        keep(k, d).start()
+    for k in order:
+        move(k, ahead(k), 2, 1).wait_recv()
+        keep(k, 2).start()
+    for k in order:
+        for d in (1, 3):
+            move(k, d, 0, d - 1).wait_send()
+        move(k, ahead(k), ahead(k), 1).wait_send()
     for swap in (q_swap, dm_swap, kv_swap):
         swap.drain()
     across.drain()
+    for store in stores:
+        store.wait()
+    for k in order:
+        for back in range(4):
+            keep(k, back).wait()
 
 
 def run_encoder(*args):
@@ -378,8 +414,11 @@
             sds((16, 256, 256), BF), sds((4, 256, 128), BF), sds((4, 256, 128), BF),
         ),
         in_specs=[VM, VM] + [ANY] * 8,
-        out_specs=(VM,) * 7,
+        out_specs=(ANY,) * 7,
         scratch_shapes=[
+            pltpu.VMEM((256, 1024), BF), pltpu.VMEM((256, 1024), F32), pltpu.VMEM((256, 1024), BF),
+            pltpu.VMEM((256, 1024), BF), pltpu.VMEM((16, 256, 256), BF), pltpu.VMEM((4, 256, 128), BF),
+            pltpu.VMEM((4, 256, 128), BF), dma((6,)), dma((4, 4)),
             pltpu.VMEM((1024, 1024), BF), pltpu.VMEM((1024, 1024), BF),
             pltpu.VMEM((1024, 512), BF), pltpu.VMEM((1024, 512), BF),
             pltpu.VMEM((256, 4096), BF), pltpu.VMEM((4096, 512), BF),
@@ -439,7 +478,7 @@
         position = origin + lax.broadcasted_iota(jnp.int32, (256, 1), 0)
 
         def score(g, m):
-            s = mm_cols(q_all[b], kv[at(g), :, pl.ds(0, 128)]) * SCALE
+            s = mm_cols(q_all[b], kv[at(g), :, pl.ds(0, 128)]) * SCALE2
             seen = (position >= begins[g]) & (position < limits[g])
             s = jnp.where(seen, s, MASKED)
             scores[g] = s
@@ -449,7 +488,7 @@
         acc[...] = jnp.zeros((256, 128), F32)
 
         def weigh(g, total):
-            p = jnp.exp(scores[g] - top)
+            p = jnp.exp2(scores[g] - top)
             scores[g] = p
             acc[...] += mm(p.astype(BF), kv[at(g), :, pl.ds(128, 128)])
             return total + jnp.sum(p, axis=1, keepdims=True)
@@ -460,14 +499,15 @@
         md[b, :, pl.ds(0, 128)] = rows.astype(BF)
         inner = jnp.sum(rows * dm_all[b].astype(F32), axis=1, keepdims=True)
         acc[...] = jnp.zeros((256, 128), F32)
+        query_t, upstream_t = q_all[b].T, dm_all[b].T
 
         def back(g, c):
             p = scores[g] * inverse
             dw = mm_cols(dm_all[b], kv[at(g), :, pl.ds(128, 128)])
             ds = (p * (dw - inner) * SCALE).astype(BF)
             acc[...] += mm(ds, kv[at(g), :, pl.ds(0, 128)])
-            d_acc[g, :, pl.ds(0, 128)] += mm_rows(ds, q_all[b])
-            d_acc[g, :, pl.ds(128, 128)] += mm_rows(p.astype(BF), dm_all[b])
+            d_acc[g, pl.ds(0, 128)] += mm(query_t, ds)
+            d_acc[g, pl.ds(128, 128)] += mm(upstream_t, p.astype(BF))
             return c
 
         lax.fori_loop(lo, hi, back, 0)
@@ -503,16 +543,18 @@
     out, first, second,
     *scratch,
 ):
-    ring_a, ring_b, ring_c = scratch[0:7], scratch[7:14], scratch[14:21]
+    ring_a, ring_b, ring_c, ring_d = scratch[0:7], scratch[7:14], scratch[14:21], scratch[21:28]
+    scratch = scratch[7:]
     v_dec, v_cot, v_attn, v_key, v_value, v_out, v_enc, v_normed, v_act, v_pre, load_sem = scratch[21:32]
     (
-        m_all, ms, mr, row_slots, zs, zr, row, kvg, ks, kr, mixed, d_query,
+        m_all, ms, mr, row_slots, passing, zs, zr, row, kvg, ks, kr, mixed, mixed_t, query_t,
         out_own, out_send, out_recv, os, orr, stage, arrived, ps, pr,
-    ) = scratch[32:53]
+    ) = scratch[32:55]
     (
         k_grad, v_grad, parts, slots, d_enc, hs1, hr1, hs2, hr2, d_pre,
-        own_b, stage_b, arrived_b, own_c, stage_c, arrived_c, cs, cr,
-    ) = scratch[53:]
+        own_b, stage_b, arrived_b, own_c1, stage_c1, arrived_c1, own_c2, stage_c2, arrived_c2, cs, cr, enc_t, normed_t, d_enc_t,
+    ) = scratch[55:]
+    own_c, stage_c, arrived_c = (own_c1, own_c2), (stage_c1, stage_c2), (arrived_c1, arrived_c2)
     greet(True)
     loads = [
         pltpu.make_async_copy(a, v, load_sem.at[i])
@@ -530,19 +572,38 @@
     m_swap = Swap(md, m_all, ms, mr)
     kv_swap = Swap(row, kvg, ks, kr)
 
+    def mine(k, d):
+        return d_kv.at[4 * ((along + d) & 3) + ((across_at + k) & 3)]
+
+    def ahead(k):
+        return 1 if k % 2 == 0 else 3
+
+    def handed(k):
+        return along_copy(ahead(k), mine(k, 2), passing.at[k], zs.at[1, k], zr.at[1, k])
+
     def term(k, d):
-        src = d_kv.at[4 * ((along + d) & 3) + ((across_at + k) & 3)]
-        return along_copy(d, src, row_slots.at[d - 1, k], zs.at[d - 1, k], zr.at[d - 1, k])
-
+        src = passing.at[k] if d == ahead(k) else mine(k, d)
+        return along_copy(d, src, row_slots.at[(d - 1) // 2, k], zs.at[d - 1, k], zr.at[d - 1, k])
+
+    order = (2, 1, 3, 0)
     m_swap.start()
-    for k in (2, 1, 3, 0):
-        for d in (2, 1, 3):
-            term(k, d).start()
+    for k in order:
+        handed(k).start()
+    for k in order:
+        term(k, 4 - ahead(k)).start()
     m_swap.keep()
+    loads[5].wait()
+    enc_t[...] = v_enc[...].T
     m_swap.finish()
     for j in range(4):
         mixed[:, pl.ds(128 * j, 128)] = m_all[j, :, pl.ds(0, 128)]
-        d_query[:, pl.ds(128 * j, 128)] = m_all[j, :, pl.ds(128, 128)]
+        mixed_t[pl.ds(128 * j, 128), :] = m_all[j, :, pl.ds(0, 128)].T
+        query_t[pl.ds(128 * j, 128), :] = m_all[j, :, pl.ds(128, 128)].T
+    for k in order:
+        handed(k).wait_recv()
+        handed(k).wait_send()
+        passing[k] = (passing[k].astype(F32) + mine(k, ahead(k))[...].astype(F32)).astype(BF)
+        term(k, ahead(k)).start()
 
     def out_copy(d):
         return head_copy(d, out_send.at[d - 1], out_recv.at[d - 1], os, orr)
@@ -555,14 +616,15 @@
         start = ((h + d) & 3) * 1024
         for n in range(4):
             out_send[d - 1, :, pl.ds(n * 256, 256)] = mm(mixed[...], v_attn[:, part(n, start)]).astype(BF)
-        out_copy(d).start()
+        if d != 2:
+            out_copy(d).start()
     loads[1].wait()
     loads[2].wait()
 
     def products(u):
         t = (u + 8 * (1 - grp)) & 15
         here = pl.ds(pl.multiple_of(t * 256, 256), 256)
-        return mm_rows(v_dec[:, here], d_query[...]), mm_rows(v_cot[:, here], mixed[...])
+        return mm(query_t[...], v_dec[:, here]), mm(mixed_t[...], v_cot[:, here])
 
     def exchange(u):
         place_u = (u >> 1, pl.ds(2 * (u & 1), 2))
@@ -571,17 +633,18 @@
     def far(u, c):
         for which, value in enumerate(products(u)):
             for k in range(2):
-                stage[u >> 1, 2 * (u & 1) + k, pl.ds(128 * which, 128)] = value[128 * k : 128 * (k + 1)].astype(BF)
+                block = 2 * (u & 1) + k
+                stage[u >> 1, block, :, pl.ds(128 * which, 128)] = value[:, 128 * k : 128 * (k + 1)].astype(BF)
         exchange(u).start()
         return c
 
     lax.fori_loop(0, 8, far, 0)
-    for k in (2, 1, 3, 0):
+    for k in order:
         there = (across_at + k) & 3
         total = d_kv[4 * along + there].astype(F32)
-        for d in (1, 3, 2):
+        for d in (4 - ahead(k), ahead(k)):
             term(k, d).wait_recv()
-            total = total + row_slots[d - 1, k].astype(F32)
+            total = total + row_slots[(d - 1) // 2, k].astype(F32)
         row[there] = total.astype(BF)
         if k:
             kv_swap.sending(k).start()
@@ -592,19 +655,23 @@
         exchange(u).wait_recv()
         for which, value in enumerate(values):
             for k in range(2):
-                rows = pl.ds(128 * which, 128)
+                cols = pl.ds(128 * which, 128)
                 block = 2 * (u & 1) + k
-                both = value[128 * k : 128 * (k + 1)] + arrived[u >> 1, block, rows].astype(F32)
-                arrived[u >> 1, block, rows] = both.astype(BF)
+                both = value[:, 128 * k : 128 * (k + 1)].astype(BF) + arrived[u >> 1, block, :, cols]
+                arrived[u >> 1, block, :, cols] = both
         return c
 
-    lax.fori_loop(0, 8, near, 0)
-    scatter_a = Scatter(arrived, 128, *ring_a)
-    scatter_a.start_all()
+    scatter_a = Scatter(arrived, 256, *ring_a)
+    lax.fori_loop(0, 4, near, 0)
+    scatter_a.start(0, 0)
+    lax.fori_loop(4, 8, near, 0)
+    scatter_a.start(1, 0)
+    scatter_a.start(0, 1)
+    scatter_a.start(1, 1)
     kv_swap.finish()
     for j in range(4):
-        k_grad[:, pl.ds(128 * j, 128)] = kvg[j, :, pl.ds(0, 128)]
-        v_grad[:, pl.ds(128 * j, 128)] = kvg[j, :, pl.ds(128, 128)]
+        k_grad[:, pl.ds(128 * j, 128)] = kvg[j, pl.ds(0, 128)].T
+        v_grad[:, pl.ds(128 * j, 128)] = kvg[j, pl.ds(128, 128)].T
     loads[3].wait()
     loads[4].wait()
     for n in range(4):
@@ -619,73 +686,76 @@
         out_own[:, pl.ds(n * 256, 256)] = mm(mixed[...], v_attn[:, here]) + v_dec[:, here].astype(F32)
     far_from, near_from = (1 - grp) * 512, grp * 512
 
-    def put(left, right, row_at, far_to, near_to):
-        for base, target in ((far_from, far_to), (near_from, near_to)):
-            for n in range(2):
-                cols = part(n, base)
-                value = mm_rows(left[:, cols], right[...])
-                for k in range(8):
-                    block = n * 8 + k
-                    target[block // 4, block % 4, pl.ds(row_at, 32)] = value[32 * k : 32 * (k + 1)].astype(BF)
+    def put(left_t, right, row_at, base, target):
+        for n in range(2):
+            value = mm(left_t[part(n, base), :], right[...])
+            for k in range(8):
+                block = n * 8 + k
+                for m in range(value.shape[1] // 512):
+                    piece = value[32 * k : 32 * (k + 1), 512 * m : 512 * (m + 1)].astype(BF)
+                    target[block // 4, block % 4, pl.ds(row_at + 32 * m, 32)] = piece
 
     def add(own, more):
         def body(b, c):
-            own[b] = (own[b].astype(F32) + more[b].astype(F32)).astype(BF)
+            own[b] = own[b] + more[b]
             return c
 
         lax.fori_loop(0, 4, body, 0)
 
-    loads[5].wait()
     swap_b = partner_copy(stage_b, arrived_b, cs.at[0], cr.at[0])
-    put(v_enc, k_grad, 0, stage_b, own_b)
-    put(v_enc, v_grad, 32, stage_b, own_b)
+    put(enc_t, k_grad, 0, far_from, stage_b)
+    put(enc_t, v_grad, 32, far_from, stage_b)
     swap_b.start()
+    put(enc_t, k_grad, 0, near_from, own_b)
+    put(enc_t, v_grad, 32, near_from, own_b)
     total_d.share(total_d.receive())
     swap_b.wait_recv()
     add(own_b, arrived_b)
     scatter_b = Scatter(own_b, 32, *ring_b)
     scatter_b.start_all()
-    total = out_own[...]
-    for d in (1, 3, 2):
-        out_copy(d).wait_recv()
-        total = total + out_recv[d - 1].astype(F32)
-    out[...] = total.astype(BF)
     for load in loads[6:]:
         load.wait()
+    normed_t[...] = v_normed[...].T
     total_d.collect()
+    out_copy(2).start()
+    d_enc_t[...] = d_enc[...].T
+    swap_c = [partner_copy(stage_c[i], arrived_c[i], cs.at[1 + i], cr.at[1 + i]) for i in range(2)]
+    put(d_enc_t, v_act, 0, far_from, stage_c[1])
+    swap_c[1].start()
     for n in range(4):
         cols = pl.ds(n * 256, 256)
         pre = v_pre[:, cols]
         sig = 1.0 / (1.0 + jnp.exp(-pre))
         slope = sig * (1.0 + pre * (1.0 - sig))
         d_pre[:, cols] = (mm_cols(d_enc[...], v_out[cols, :]) * slope).astype(BF)
-    halves = [pl.ds(64 * which, 64) for which in range(2)]
-    swap_c = [
-        partner_copy(stage_c.at[:, :, r], arrived_c.at[:, :, r], cs.at[1 + i], cr.at[1 + i])
-        for i, r in enumerate(halves)
-    ]
-    for n in range(2):
-        put(d_enc, v_act.at[:, pl.ds(512 * n, 512)], 64 + 32 * n, stage_c, own_c)
-    swap_c[1].start()
-    for n in range(2):
-        put(v_normed, d_pre.at[:, pl.ds(512 * n, 512)], 32 * n, stage_c, own_c)
+    put(normed_t, d_pre, 0, far_from, stage_c[0])
     swap_c[0].start()
+    scatters_c = [Scatter(own_c[i], 32, *rings) for i, rings in enumerate((ring_c, ring_d))]
+    put(d_enc_t, v_act, 0, near_from, own_c[1])
+    swap_c[1].wait_recv()
+    add(own_c[1], arrived_c[1])
+    scatters_c[1].start_all()
+    put(normed_t, d_pre, 0, near_from, own_c[0])
+    swap_c[0].wait_recv()
+    add(own_c[0], arrived_c[0])
+    scatters_c[0].start_all()
     scatter_a.middle()
-    for copy in (swap_c[1], swap_c[0]):
-        copy.wait_recv()
-    add(own_c, arrived_c)
-    scatter_c = Scatter(own_c, 64, *ring_c)
-    scatter_c.start_all()
     scatter_b.middle()
     for half in range(2):
-        first[pl.ds(128 * half, 128)] = scatter_a.finish(half)
+        first[pl.ds(256 * half, 256)] = scatter_a.finish(half)
     for half in range(2):
         second[pl.ds(32 * half, 32)] = scatter_b.finish(half)
-    scatter_c.middle()
+    scatters_c[1].middle()
+    scatters_c[0].middle()
+    total = out_own[...]
+    for d in (1, 3, 2):
+        out_copy(d).wait_recv()
+        total = total + out_recv[d - 1].astype(F32)
+    out[...] = total.astype(BF)
     m_swap.drain()
     kv_swap.drain()
     for k in range(4):
-        for d in (1, 2, 3):
+        for d in (1, 3):
             term(k, d).wait_send()
     for d in (1, 2, 3):
         out_copy(d).wait_send()
@@ -700,9 +770,11 @@
     total_d.drain()
     for copy in (swap_b, *swap_c):
         copy.wait_send()
-    for half in range(2):
-        second[pl.ds(64 + 64 * half, 64)] = scatter_c.finish(half)
-    scatter_c.drain()
+    for i in (1, 0):
+        for half in range(2):
+            second[pl.ds(64 + 64 * i + 32 * half, 32)] = scatters_c[i].finish(half)
+    for scatter in scatters_c:
+        scatter.drain()
 
 
 def run_decoder(*args):
@@ -710,28 +782,29 @@
     dma = pltpu.SemaphoreType.DMA
     return pl.pallas_call(
         decoder_kernel,
-        out_shape=(sds((256, 1024), BF), sds((256, 512), F32), sds((192, 512), F32)),
+        out_shape=(sds((256, 1024), BF), sds((512, 256), F32), sds((192, 512), F32)),
         in_specs=[VM, VM] + [ANY] * 10,
         out_specs=(VM,) * 3,
         scratch_shapes=[
-            *Scatter.scratch(128), *Scatter.scratch(32), *Scatter.scratch(64),
+            *Scatter.scratch(256, 256), *Scatter.scratch(32, 512), *Scatter.scratch(32, 512), *Scatter.scratch(32, 512),
             pltpu.VMEM((256, 4096), BF), pltpu.VMEM((256, 4096), BF), pltpu.VMEM((512, 4096), BF),
             pltpu.VMEM((1024, 512), BF), pltpu.VMEM((1024, 512), BF), pltpu.VMEM((1024, 1024), BF),
             pltpu.VMEM((256, 1024), BF), pltpu.VMEM((256, 1024), BF), pltpu.VMEM((256, 1024), BF),
             pltpu.VMEM((256, 1024), F32), dma((10,)),
             pltpu.VMEM((4, 256, 256), BF), dma((3,)), dma((3,)),
-            pltpu.VMEM((3, 4, 256, 256), BF), dma((3, 4)), dma((3, 4)),
+            pltpu.VMEM((2, 4, 256, 256), BF), pltpu.VMEM((4, 256, 256), BF), dma((3, 4)), dma((3, 4)),
             pltpu.VMEM((4, 256, 256), BF), pltpu.VMEM((4, 256, 256), BF), dma((3,)), dma((3,)),
-            pltpu.VMEM((256, 512), BF), pltpu.VMEM((256, 512), BF),
+            pltpu.VMEM((256, 512), BF), pltpu.VMEM((512, 256), BF), pltpu.VMEM((512, 256), BF),
             pltpu.VMEM((256, 1024), F32), pltpu.VMEM((3, 256, 1024), BF), pltpu.VMEM((3, 256, 1024), BF),
             dma((3,)), dma((3,)),
-            pltpu.VMEM((4, 4, 256, 512), BF), pltpu.VMEM((4, 4, 256, 512), BF), dma((8,)), dma((8,)),
+            pltpu.VMEM((4, 4, 512, 256), BF), pltpu.VMEM((4, 4, 512, 256), BF), dma((8,)), dma((8,)),
             pltpu.VMEM((256, 512), BF), pltpu.VMEM((256, 512), BF),
             pltpu.VMEM((256, 1024), BF), pltpu.VMEM((3, 64, 1024), BF), pltpu.VMEM((256, 1024), BF),
             dma((3,)), dma((3,)), dma((3,)), dma((3,)),
             pltpu.VMEM((256, 1024), BF),
-            *[pltpu.VMEM((4, 4, 64, 512), BF)] * 3, *[pltpu.VMEM((4, 4, 128, 512), BF)] * 3,
+            *[pltpu.VMEM((4, 4, 64, 512), BF)] * 9,
             dma((3,)), dma((3,)),
+            *[pltpu.VMEM((1024, 256), BF)] * 3,
         ],
         compiler_params=pltpu.CompilerParams(
             collective_id=1, has_side_effects=True, vmem_limit_bytes=VMEM_LIMIT
@@ -743,8 +816,8 @@
 
 def unpack_kernel(first, second, out_in, out, g_query, g_key, g_value, g_attn, g_in, g_out):
     out[...] = out_in[...]
-    g_query[...] = first[pl.ds(0, 128)]
-    g_attn[...] = first[pl.ds(128, 128)].T
+    g_query[...] = first[:, pl.ds(0, 128)].T
+    g_attn[...] = first[:, pl.ds(128, 128)]
     g_key[...] = second[pl.ds(0, 32)]
     g_value[...] = second[pl.ds(32, 32)]
     for n in range(2):

time: 153 us -> 146 us (0.954); the launches traced: 153 us -> 145 us
  Pallas kernels: 153 us -> 144 us
    pallas_call x1, Pallas kernels: 25 us -> 12.8 us  [run_attention(): pl.pallas_call(attention_kernel, out_shape=(sds((4, 256, 256), BF), sds((...]
    pallas_call x1, Pallas kernels: 78.7 us -> 85.6 us  [run_decoder(): pl.pallas_call(decoder_kernel, out_shape=(sds((256, 1024), BF), sds((512,...]
    pallas_call x1, Pallas kernels: 46.4 us -> 43.1 us  [run_encoder(): pl.pallas_call(encoder_kernel, out_shape=(sds((256, 1024), BF), sds((256,...]
where the time goes in v4:
time: 146 us; the launch traced here: 145 us
  Pallas kernels  144 us (99%)
    pallas_call x1, Pallas kernels, run_decoder(): pl.pallas_call(decoder_kernel, out_shape=(sds((256, 1024), BF), sds((512,...  85.6 us
    pallas_call x1, Pallas kernels, run_encoder(): pl.pallas_call(encoder_kernel, out_shape=(sds((256, 1024), BF), sds((256,...  43.1 us
    pallas_call x1, Pallas kernels, run_attention(): pl.pallas_call(attention_kernel, out_shape=(sds((4, 256, 256), BF), sds((...  12.8 us

profile of v4, /device:TPU:0, one launch (start us, length us, event | category | flops | bytes accessed | tf_op | source)
XLA Modules:
  0.0 144.6 jit_solution(7436574530461685996)
XLA Ops:
  0.6 43.1 %encoder_gather.1 = (bf16[256,1024]{1,0:T(8,128)(2,1)}, f32[256,1024]{1,0:T(8,128)}, bf16[256,1024]{1,0:T(8,128)(2,1)}, bf16[256,1024]{1,0:T(8,128)(2,1)}, bf16[...) custom-call(bf16[256,1024]{1,0:T(8,128)(2,1)} %bitcast.10, ...), custom_call_target="tpu_custom_call" | custom-call | flops 5000000000 | bytes 25165824 | tf_op jit(solution)/shard_map/encoder_gather/pallas_call | solution.py:410
  43.7 12.8 %attention.1 = (bf16[4,256,256]{2,1,0:T(8,128)(2,1)}, bf16[16,256,256]{2,1,0:T(8,128)(2,1)}) custom-call(s32[1,16]{1,0:T(1,128)} %group_doc.1, s32[1,8]{1,0:T(1,128)} %doc_lengths.1, bf16[4,256,128]{2,1,0:T(8,128)(2,1)} %get-tuple-element.26.q_all, bf16[4,256,128]{2,1,0:T(8,128)(2,1)} %get-tuple-element.27.dm_all, bf16[16,256,256]{2,1,0:T(8,128)(2,1)} %get-tuple-element.28.kv), custom_call_target="tpu_custom_call" | custom-call | flops 2000000000 | bytes 6291456 | tf_op jit(solution)/shard_map/attention/pallas_call | solution.py:526
  56.5 85.6 %decoder_scatter.1 = (bf16[256,1024]{1,0:T(8,128)(2,1)}, f32[512,256]{1,0:T(8,128)}, f32[192,512]{1,0:T(8,128)}) custom-call(bf16[16,256,256]{2,1,0:T(8,128)(2,1)} %get-tuple-element.29.d_kv, bf16[4,256,256]{2,1,0:T(8,128)(2,1)} %get-tuple-element.30.md, bf16[256,4096]{1,0:T(8,128)(2,1)} %bitcast.7, bf16[256,4096]{1,0:T(8,128)(2,1)} %bitcast.9, ...), custom_call_target="tpu_custom_call" | custom-call | flops 7000000000 | bytes 25165824 | tf_op jit(solution)/shard_map/decoder_scatter/pallas_call | solution.py:783
  142.2 2.4 %unpack.1 = (bf16[256,1024]{1,0:T(8,128)(2,1)}, f32[128,512]{1,0:T(8,128)}, f32[32,512]{1,0:T(8,128)}, f32[32,512]{1,0:T(8,128)}, f32[512,128]{1,0:T(8,128)}, /*index=5*/f32[32,1024]{1,0:T(8,128)}, f32[32,1024]{1,0:T(8,128)}) custom-call(f32[512,256]{1,0:T(8,128)} %get-tuple-element.35.first, f32[192,512]{1,0:T(8,128)} %get-tuple-element.36.second, ...), custom_call_target="tpu_custom_call" | custom-call | tf_op jit(solution)/shard_map/unpack/pallas_call | solution.py:831

commit v5 on v4

--- a/solution.py
+++ b/solution.py
@@ -145,9 +145,9 @@
 
 
 class Scatter:
-    def __init__(self, blocks, n, slots, sums, last, ss, rs, ss2, rs2):
+    def __init__(self, blocks, n, slots, passing, sums, last, ss, rs, ss2, rs2):
         self.blocks, self.n = blocks, n
-        self.slots, self.sums, self.last = slots, sums, last
+        self.slots, self.passing, self.sums, self.last = slots, passing, sums, last
         self.ss, self.rs, self.ss2, self.rs2 = ss, rs, ss2, rs2
         self.z, self.x = place()
 
@@ -158,10 +158,21 @@
             return self.blocks.at[two, (self.x + d) & 3, rows]
         return self.blocks.at[(self.z + d) & 3, two, rows]
 
+    def ahead(self, chunk):
+        return 3 if chunk else 1
+
+    def handed(self, half, chunk):
+        move = x_copy if half == 0 else z_copy
+        return move(
+            self.ahead(chunk), self.cut(half, 2, chunk), self.passing.at[half, chunk],
+            self.ss.at[half, 1, chunk], self.rs.at[half, 1, chunk],
+        )
+
     def first(self, half, d, chunk):
         move = x_copy if half == 0 else z_copy
+        src = self.passing.at[half, chunk] if d == self.ahead(chunk) else self.cut(half, d, chunk)
         return move(
-            d, self.cut(half, d, chunk), self.slots.at[half, d - 1, pl.ds(2 * chunk, 2)],
+            d, src, self.slots.at[half, (d - 1) // 2, pl.ds(2 * chunk, 2)],
             self.ss.at[half, d - 1, chunk], self.rs.at[half, d - 1, chunk],
         )
 
@@ -174,8 +185,17 @@
         )
 
     def start(self, half, chunk):
-        for d in (2, 1, 3):
-            self.first(half, d, chunk).start()
+        self.handed(half, chunk).start()
+        self.first(half, 4 - self.ahead(chunk), chunk).start()
+
+    def relay(self):
+        for chunk in (0, 1):
+            for half in (0, 1):
+                self.handed(half, chunk).wait()
+                own = self.cut(half, self.ahead(chunk), chunk)
+                for k in range(2):
+                    self.passing[half, chunk, k] = self.passing[half, chunk, k] + own[k]
+                self.first(half, self.ahead(chunk), chunk).start()
 
     def start_all(self):
         for chunk in (0, 1):
@@ -185,12 +205,12 @@
     def middle(self, halves=(0, 1)):
         for half in halves:
             for chunk in (0, 1):
-                for d in (1, 3, 2):
+                for d in (4 - self.ahead(chunk), self.ahead(chunk)):
                     self.first(half, d, chunk).wait_recv()
                 own = self.cut(half, 0, chunk)
                 for k in range(2):
                     total = own[k].astype(F32)
-                    for d in range(3):
+                    for d in range(2):
                         total = total + self.slots[half, d, 2 * chunk + k].astype(F32)
                     self.sums[half, 2 * chunk + k] = total.astype(BF)
             for d in (2, 1, 3):
@@ -207,16 +227,17 @@
 
     def drain(self):
         for half in (0, 1):
+            for chunk in (0, 1):
+                for d in (1, 3):
+                    self.first(half, d, chunk).wait_send()
             for d in (1, 2, 3):
-                for chunk in (0, 1):
-                    self.first(half, d, chunk).wait_send()
                 self.second(half, d).wait_send()
 
     @staticmethod
     def scratch(n, c):
         dma = pltpu.SemaphoreType.DMA
         return [
-            pltpu.VMEM((2, 3, 4, n, c), BF), pltpu.VMEM((2, 4, n, c), BF), pltpu.VMEM((2, 3, n, c), BF),
+            pltpu.VMEM((2, 2, 4, n, c), BF), pltpu.VMEM((2, 2, 2, n, c), BF), pltpu.VMEM((2, 4, n, c), BF), pltpu.VMEM((2, 3, n, c), BF),
             dma((2, 3, 2)), dma((2, 3, 2)), dma((2, 3)), dma((2, 3)),
         ]
 
@@ -477,40 +498,58 @@
         origin, lo, hi = bounds[b]
         position = origin + lax.broadcasted_iota(jnp.int32, (256, 1), 0)
 
-        def score(g, m):
+        steps = (hi - lo + 1) >> 1
+
+        def pair(i):
+            g = lo + 2 * i
+            return g, jnp.minimum(g + 1, N_SEQ - 1), g + 1 < hi
+
+        def score(g, valid):
             s = mm_cols(q_all[b], kv[at(g), :, pl.ds(0, 128)]) * SCALE2
-            seen = (position >= begins[g]) & (position < limits[g])
-            s = jnp.where(seen, s, MASKED)
-            scores[g] = s
-            return jnp.maximum(m, jnp.max(s, axis=1, keepdims=True))
-
-        top = lax.fori_loop(lo, hi, score, jnp.full((256, 1), MASKED, F32))
+            first = begins[g] if valid is None else jnp.where(valid, begins[g], 1 << 30)
+            return jnp.where((position >= first) & (position < limits[g]), s, MASKED)
+
         acc[...] = jnp.zeros((256, 128), F32)
 
-        def weigh(g, total):
-            p = jnp.exp2(scores[g] - top)
-            scores[g] = p
-            acc[...] += mm(p.astype(BF), kv[at(g), :, pl.ds(128, 128)])
-            return total + jnp.sum(p, axis=1, keepdims=True)
-
-        total = lax.fori_loop(lo, hi, weigh, jnp.zeros((256, 1), F32))
-        inverse = 1.0 / total
-        rows = acc[...] * inverse
+        def weigh(i, carry):
+            top, total = carry
+            g, other, valid = pair(i)
+            s, r = score(g, None), score(other, valid)
+            scores[2 * i], scores[2 * i + 1] = s, r
+            peak = jnp.maximum(top, jnp.max(jnp.maximum(s, r), axis=1, keepdims=True))
+            shrink = jnp.exp2(top - peak)
+            p, o = jnp.exp2(s - peak), jnp.exp2(r - peak)
+            more = mm(p.astype(BF), kv[at(g), :, pl.ds(128, 128)])
+            more = more + mm(o.astype(BF), kv[at(other), :, pl.ds(128, 128)])
+            acc[...] = acc[...] * shrink + more
+            return peak, total * shrink + jnp.sum(p + o, axis=1, keepdims=True)
+
+        start = (jnp.full((256, 1), MASKED, F32), jnp.zeros((256, 1), F32))
+        top, total = lax.fori_loop(0, steps, weigh, start)
+        rows = acc[...] / total
+        level = top + jnp.log2(total)
         md[b, :, pl.ds(0, 128)] = rows.astype(BF)
         inner = jnp.sum(rows * dm_all[b].astype(F32), axis=1, keepdims=True)
         acc[...] = jnp.zeros((256, 128), F32)
         query_t, upstream_t = q_all[b].T, dm_all[b].T
 
-        def back(g, c):
-            p = scores[g] * inverse
-            dw = mm_cols(dm_all[b], kv[at(g), :, pl.ds(128, 128)])
-            ds = (p * (dw - inner) * SCALE).astype(BF)
-            acc[...] += mm(ds, kv[at(g), :, pl.ds(0, 128)])
-            d_acc[g, pl.ds(0, 128)] += mm(query_t, ds)
-            d_acc[g, pl.ds(128, 128)] += mm(upstream_t, p.astype(BF))
+        def back(i, c):
+            g, other, _ = pair(i)
+            more = acc[...]
+            terms = []
+            for n, at_g in ((0, g), (1, other)):
+                p = jnp.exp2(scores[2 * i + n] - level)
+                dw = mm_cols(dm_all[b], kv[at(at_g), :, pl.ds(128, 128)])
+                ds = (p * (dw - inner) * SCALE).astype(BF)
+                more = more + mm(ds, kv[at(at_g), :, pl.ds(0, 128)])
+                terms.append((at_g, mm(query_t, ds), mm(upstream_t, p.astype(BF))))
+            acc[...] = more
+            for at_g, d_key, d_value in terms:
+                d_acc[at_g, pl.ds(0, 128)] += d_key
+                d_acc[at_g, pl.ds(128, 128)] += d_value
             return c
 
-        lax.fori_loop(lo, hi, back, 0)
+        lax.fori_loop(0, steps, back, 0)
         md[b, :, pl.ds(128, 128)] = acc[...].astype(BF)
 
     def settle(g, c):
@@ -543,8 +582,8 @@
     out, first, second,
     *scratch,
 ):
-    ring_a, ring_b, ring_c, ring_d = scratch[0:7], scratch[7:14], scratch[14:21], scratch[21:28]
-    scratch = scratch[7:]
+    ring_a, ring_b, ring_c, ring_d = (scratch[8 * i : 8 * i + 8] for i in range(4))
+    scratch = scratch[11:]
     v_dec, v_cot, v_attn, v_key, v_value, v_out, v_enc, v_normed, v_act, v_pre, load_sem = scratch[21:32]
     (
         m_all, ms, mr, row_slots, passing, zs, zr, row, kvg, ks, kr, mixed, mixed_t, query_t,
@@ -611,13 +650,6 @@
     def part(n, start):
         return pl.ds(pl.multiple_of(start + n * 256, 256), 256)
 
-    loads[0].wait()
-    for d in (2, 1, 3):
-        start = ((h + d) & 3) * 1024
-        for n in range(4):
-            out_send[d - 1, :, pl.ds(n * 256, 256)] = mm(mixed[...], v_attn[:, part(n, start)]).astype(BF)
-        if d != 2:
-            out_copy(d).start()
     loads[1].wait()
     loads[2].wait()
 
@@ -680,6 +712,11 @@
         parts[:, rows] = value.astype(BF)
     total_d = HeadSum(parts, slots, d_enc, hs1, hr1, hs2, hr2)
     total_d.send()
+    loads[0].wait()
+    for d in (2, 1, 3):
+        start = ((h + d) & 3) * 1024
+        for n in range(4):
+            out_send[d - 1, :, pl.ds(n * 256, 256)] = mm(mixed[...], v_attn[:, part(n, start)]).astype(BF)
 
     for n in range(4):
         here = part(n, h * 1024)
@@ -709,6 +746,7 @@
     put(enc_t, k_grad, 0, near_from, own_b)
     put(enc_t, v_grad, 32, near_from, own_b)
     total_d.share(total_d.receive())
+    scatter_a.relay()
     swap_b.wait_recv()
     add(own_b, arrived_b)
     scatter_b = Scatter(own_b, 32, *ring_b)
@@ -717,7 +755,8 @@
         load.wait()
     normed_t[...] = v_normed[...].T
     total_d.collect()
-    out_copy(2).start()
+    for d in (1, 3, 2):
+        out_copy(d).start()
     d_enc_t[...] = d_enc[...].T
     swap_c = [partner_copy(stage_c[i], arrived_c[i], cs.at[1 + i], cr.at[1 + i]) for i in range(2)]
     put(d_enc_t, v_act, 0, far_from, stage_c[1])
@@ -728,6 +767,7 @@
         sig = 1.0 / (1.0 + jnp.exp(-pre))
         slope = sig * (1.0 + pre * (1.0 - sig))
         d_pre[:, cols] = (mm_cols(d_enc[...], v_out[cols, :]) * slope).astype(BF)
+    scatter_b.relay()
     put(normed_t, d_pre, 0, far_from, stage_c[0])
     swap_c[0].start()
     scatters_c = [Scatter(own_c[i], 32, *rings) for i, rings in enumerate((ring_c, ring_d))]
@@ -736,10 +776,12 @@
     add(own_c[1], arrived_c[1])
     scatters_c[1].start_all()
     put(normed_t, d_pre, 0, near_from, own_c[0])
+    scatters_c[1].relay()
     swap_c[0].wait_recv()
     add(own_c[0], arrived_c[0])
     scatters_c[0].start_all()
     scatter_a.middle()
+    scatters_c[0].relay()
     scatter_b.middle()
     for half in range(2):
         first[pl.ds(256 * half, 256)] = scatter_a.finish(half)

time: 146 us -> 138 us (0.945); the launches traced: 145 us -> 139 us
  Pallas kernels: 144 us -> 138 us
    pallas_call x1, Pallas kernels: 85.6 us -> 80.7 us  [run_decoder(): pl.pallas_call(decoder_kernel, out_shape=(sds((256, 1024), BF), sds((512,...]
where the time goes in v5:
time: 138 us; the launch traced here: 139 us
  Pallas kernels  138 us (100%)
    pallas_call x1, Pallas kernels, run_decoder(): pl.pallas_call(decoder_kernel, out_shape=(sds((256, 1024), BF), sds((512,...  80.7 us
    pallas_call x1, Pallas kernels, run_encoder(): pl.pallas_call(encoder_kernel, out_shape=(sds((256, 1024), BF), sds((256,...  43.1 us
    pallas_call x1, Pallas kernels, run_attention(): pl.pallas_call(attention_kernel, out_shape=(sds((4, 256, 256), BF), sds((...  11.7 us

profile of v5, /device:TPU:0, one launch (start us, length us, event | category | flops | bytes accessed | tf_op | source)
XLA Modules:
  0.0 138.6 jit_solution(5861601239211924338)
XLA Ops:
  0.6 43.1 %encoder_gather.1 = (bf16[256,1024]{1,0:T(8,128)(2,1)}, f32[256,1024]{1,0:T(8,128)}, bf16[256,1024]{1,0:T(8,128)(2,1)}, bf16[256,1024]{1,0:T(8,128)(2,1)}, bf16[...) custom-call(bf16[256,1024]{1,0:T(8,128)(2,1)} %bitcast.10, ...), custom_call_target="tpu_custom_call" | custom-call | flops 5000000000 | bytes 25165824 | tf_op jit(solution)/shard_map/encoder_gather/pallas_call | solution.py:431
  43.7 11.7 %attention.1 = (bf16[4,256,256]{2,1,0:T(8,128)(2,1)}, bf16[16,256,256]{2,1,0:T(8,128)(2,1)}) custom-call(s32[1,16]{1,0:T(1,128)} %group_doc.1, s32[1,8]{1,0:T(1,128)} %doc_lengths.1, bf16[4,256,128]{2,1,0:T(8,128)(2,1)} %get-tuple-element.26.q_all, bf16[4,256,128]{2,1,0:T(8,128)(2,1)} %get-tuple-element.27.dm_all, bf16[16,256,256]{2,1,0:T(8,128)(2,1)} %get-tuple-element.28.kv), custom_call_target="tpu_custom_call" | custom-call | flops 2000000000 | bytes 6291456 | tf_op jit(solution)/shard_map/attention/pallas_call | solution.py:565
  55.5 80.7 %decoder_scatter.1 = (bf16[256,1024]{1,0:T(8,128)(2,1)}, f32[512,256]{1,0:T(8,128)}, f32[192,512]{1,0:T(8,128)}) custom-call(bf16[16,256,256]{2,1,0:T(8,128)(2,1)} %get-tuple-element.29.d_kv, bf16[4,256,256]{2,1,0:T(8,128)(2,1)} %get-tuple-element.30.md, bf16[256,4096]{1,0:T(8,128)(2,1)} %bitcast.7, bf16[256,4096]{1,0:T(8,128)(2,1)} %bitcast.9, ...), custom_call_target="tpu_custom_call" | custom-call | flops 7000000000 | bytes 25165824 | tf_op jit(solution)/shard_map/decoder_scatter/pallas_call | solution.py:825
  136.1 2.4 %unpack.1 = (bf16[256,1024]{1,0:T(8,128)(2,1)}, f32[128,512]{1,0:T(8,128)}, f32[32,512]{1,0:T(8,128)}, f32[32,512]{1,0:T(8,128)}, f32[512,128]{1,0:T(8,128)}, /*index=5*/f32[32,1024]{1,0:T(8,128)}, f32[32,1024]{1,0:T(8,128)}) custom-call(f32[512,256]{1,0:T(8,128)} %get-tuple-element.35.first, f32[192,512]{1,0:T(8,128)} %get-tuple-element.36.second, ...), custom_call_target="tpu_custom_call" | custom-call | tf_op jit(solution)/shard_map/unpack/pallas_call | solution.py:873
